TPU v7x, 256 devices: a whole 4x4x8 slice. The times are simulated.
256 devices in a mesh: pipe: 8 (over y, x_lo), expert: 32 (over x_hi, z, core).
Axes of the slice: x: 4 (x_hi: 2, x_lo: 2; x = x_hi * 2 + x_lo), y: 4, z: 8, core: 2. Of those that a mesh axis runs over, the one named last changes fastest.
Arguments:
- acts_a: bfloat16 [8, 2048, 7168], P('pipe', 'expert'), may hold values from -6 to 6
- acts_b: bfloat16 [8, 2048, 7168], P('pipe', 'expert'), may hold values from -6 to 6
- cot_b: bfloat16 [8, 2048, 7168], P('pipe', 'expert'), may hold values from -1.5 to 1.5
- routes_a: int32 [8, 2048, 2], P('pipe', 'expert'), may hold values from 0 to 3, all different within a row; in each aligned block of 64 rows (0 to 63, 64 to 127, ..., all dimensions but the last counted through in order) at most 34 rows name the same one
- gates_a: float32 [8, 2048, 2], P('pipe', 'expert'), may hold values from 0.1 to 1
- routes_b: int32 [8, 2048, 2], P('pipe', 'expert'), may hold values from 0 to 3, all different within a row; in each aligned block of 64 rows (0 to 63, 64 to 127, ..., all dimensions but the last counted through in order) at most 34 rows name the same one
- gates_b: float32 [8, 2048, 2], P('pipe', 'expert'), may hold values from 0.1 to 1
- up_weight: bfloat16 [8, 28672, 1024], P('pipe', 'expert'), may hold values from -0.0625 to 0.0625
- down_weight: bfloat16 [8, 1024, 28672], P('pipe', None, 'expert'), may hold values from -0.1875 to 0.1875
- up_scale: float32 [8, 4], P('pipe'), may hold values from 0.002362278 to 0.004724556
- down_scale: float32 [8, 4], P('pipe'), may hold values from 0.00625 to 0.0125
Outputs:
- next_a: bfloat16 [8, 2048, 7168], P('pipe', 'expert')
- next_cot_b: bfloat16 [8, 2048, 7168], P('pipe', 'expert')
- up_grad: bfloat16 [8, 28672, 1024], P('pipe', 'expert')
- down_grad: bfloat16 [8, 1024, 28672], P('pipe', None, 'expert')
- up_scale_grad: float32 [8, 4], P('pipe')
- down_scale_grad: float32 [8, 4], P('pipe')
Inputs may be any that keep to these rules, and one draw needn't show every extreme that they name: `routes_a`: within the rows of one device no expert is chosen by more than 34 rows, and some expert is chosen by exactly 34 rows there. `routes_b`: within the rows of one device no expert is chosen by more than 34 rows, and some expert is chosen by exactly 34 rows there.
All inputs are finite; a program needn't handle non-finite values.
Results may differ from a plain program's by a relative error of at most 0.0091.
Values may be sent and summed in bfloat16 or wider, within the bound.
A program may use at most 128 MiB of HBM per device.

v0:
```python
import math

import jax
import jax.numpy as jnp
from jax import lax
from jax.sharding import PartitionSpec as P

D = 7168
HID = 1024
EXPERTS = 4
CAP = 34


qlimit = 7.0
epsilon = 1e-06
two_pi = 2.0 * math.pi
highest = lax.Precision.HIGHEST


def partner_2(value, axis, bit):
    return lax.ppermute(value, axis, [(i, i ^ 1 << bit) for i in range(lax.axis_size(axis))])


def passed_along(value, axis, by):
    peers = lax.axis_size(axis)
    pairs = [(i, i + by) for i in range(peers) if 0 <= i + by < peers]
    return lax.ppermute(value, axis, pairs)


def rms_norm(values):
    return values * lax.rsqrt(jnp.mean(values * values, axis=-1, keepdims=True) + epsilon)


def soft_round(values):
    return values - jnp.sin(two_pi * values) / two_pi


def fake_quant(weights, scale):
    ratio = weights.astype(jnp.float32) / scale
    return scale * soft_round(jnp.clip(ratio, -qlimit, qlimit))


def quant_grads(weights, scale, grads):
    ratio = weights.astype(jnp.float32) / scale
    inside = jnp.abs(ratio) < qlimit
    wave = 1.0 - jnp.cos(two_pi * ratio)
    grads_wide = grads.astype(jnp.float32)
    weight_grad = grads_wide * jnp.where(inside, wave, 0.0)
    slope = soft_round(jnp.clip(ratio, -qlimit, qlimit)) - jnp.where(inside, ratio * wave, 0.0)
    scale_grad = jnp.sum(grads_wide * slope) / math.sqrt(D * HID * qlimit)
    return (weight_grad, scale_grad)


def silu_grad(values):
    sigma_v = jax.nn.sigmoid(values)
    return sigma_v * (1.0 + values * (1.0 - sigma_v))


def route_tables(routes, gates):
    flat_ids = routes.reshape(-1)
    entries = flat_ids.shape[0]
    chosen = routes.shape[1]
    matches = (flat_ids[:, None] == jnp.arange(EXPERTS, dtype=jnp.int32)[None, :]).astype(jnp.int32)
    before = jnp.cumsum(matches, axis=0) - matches
    slot_of = jnp.sum(before * matches, axis=1)
    at_slot = (slot_of[:, None] == jnp.arange(CAP, dtype=jnp.int32)[None, :]).astype(jnp.float32)
    owner_of = (
        (jnp.arange(entries, dtype=jnp.int32) // chosen)[:, None]
        == jnp.arange(routes.shape[0], dtype=jnp.int32)[None, :]
    ).astype(jnp.float32)
    matches_wide = matches.astype(jnp.float32)
    dispatch = jnp.einsum("re,rc,rt->ect", matches_wide, at_slot, owner_of, precision=highest)
    weighted = jnp.einsum(
        "re,rc,rt->ect",
        matches_wide * gates.reshape(-1)[:, None],
        at_slot,
        owner_of,
        precision=highest,
    )
    return (dispatch, weighted)


def pack_rows(values, table, split_count):
    shaped = values.reshape(values.shape[0], split_count, -1)
    packed = jnp.einsum(
        "ect,tsd->escd", table.astype(jnp.bfloat16), shaped, preferred_element_type=jnp.float32
    )
    return packed.astype(jnp.bfloat16).reshape(EXPERTS * split_count, CAP, -1)


def pack_scaled(values, table, split_count):
    shaped = values.astype(jnp.float32).reshape(values.shape[0], split_count, -1)
    packed = jnp.einsum("ect,tsd->escd", table, shaped, precision=highest)
    return packed.astype(jnp.bfloat16).reshape(EXPERTS * split_count, CAP, -1)


def unpack_rows(returned, table, split_count):
    shaped = returned.astype(jnp.float32).reshape(EXPERTS, split_count, CAP, -1)
    summed = jnp.einsum("ect,escd->tsd", table, shaped, precision=highest)
    return summed.reshape(summed.shape[0], -1)


def shards(
    acts_a,
    acts_b,
    cot_b,
    routes_a,
    gates_a,
    routes_b,
    gates_b,
    up_weight,
    down_weight,
    up_scale,
    down_scale,
):
    split_count = lax.axis_size("expert") // EXPERTS
    split_bits = split_count.bit_length() - 1
    device_id = lax.axis_index("expert")
    expert_id = device_id // split_count
    part_id = device_id % split_count
    is_mine = (jnp.arange(EXPERTS, dtype=jnp.int32) == expert_id).astype(jnp.float32)
    s_up = jnp.sum(is_mine * up_scale[0])
    s_down = jnp.sum(is_mine * down_scale[0])
    w_up = up_weight[0]
    w_down = down_weight[0]
    q_up = fake_quant(w_up, s_up).astype(jnp.bfloat16)
    q_down = fake_quant(w_down, s_down).astype(jnp.bfloat16)
    part_width = w_up.shape[0]
    contract_last = (((1,), (1,)), ((), ()))
    contract_first = (((0,), (0,)), ((), ()))
    bit_order = list(range(split_bits))

    def part_sum(partial_value):
        current = partial_value
        for bit_no in bit_order:
            half_cols = current.shape[1] // 2
            upper_side = part_id >> bit_no & 1 == 1
            lower_part = current[:, :half_cols]
            upper_part = current[:, half_cols:]
            keep_part = jnp.where(upper_side, upper_part, lower_part)
            give_part = jnp.where(upper_side, lower_part, upper_part)
            current = keep_part + partner_2(give_part, "expert", bit_no)
        current = current.astype(jnp.bfloat16)
        for bit_no in reversed(bit_order):
            partner = partner_2(current, "expert", bit_no)
            upper_side = part_id >> bit_no & 1 == 1
            current = jnp.concatenate(
                (jnp.where(upper_side, partner, current), jnp.where(upper_side, current, partner)),
                axis=1,
            )
        return current

    x_a = acts_a[0]
    normed_a = rms_norm(x_a.astype(jnp.float32)).astype(jnp.bfloat16)
    disp_a, comb_a = route_tables(routes_a[0], gates_a[0])
    arrived_a = lax.all_to_all(
        pack_rows(normed_a, disp_a, split_count), "expert", split_axis=0, concat_axis=0, tiled=True
    )
    rows_in = arrived_a.reshape(-1, part_width)
    pre_a = part_sum(jnp.dot(rows_in, q_up, preferred_element_type=jnp.float32))
    hidden_a = jax.nn.silu(pre_a.astype(jnp.float32)).astype(jnp.bfloat16)
    outputs = jnp.dot(hidden_a, q_down, preferred_element_type=jnp.float32).astype(jnp.bfloat16)
    returned_a = lax.all_to_all(
        outputs.reshape(arrived_a.shape), "expert", split_axis=0, concat_axis=0, tiled=True
    )
    out_a = (x_a.astype(jnp.float32) + unpack_rows(returned_a, comb_a, split_count)).astype(
        jnp.bfloat16
    )
    x_b = acts_b[0].astype(jnp.float32)
    normed_wide, norm_back = jax.vjp(rms_norm, x_b)
    disp_b, comb_b = route_tables(routes_b[0], gates_b[0])
    send_u = pack_rows(normed_wide.astype(jnp.bfloat16), disp_b, split_count)
    send_c = pack_scaled(cot_b[0], comb_b, split_count)
    arrived_u, arrived_c = (
        lax.all_to_all(send_u, "expert", split_axis=0, concat_axis=0, tiled=True),
        lax.all_to_all(send_c, "expert", split_axis=0, concat_axis=0, tiled=True),
    )
    rows_u = arrived_u.reshape(-1, part_width)
    rows_c = arrived_c.reshape(-1, part_width)
    pre_b = part_sum(jnp.dot(rows_u, q_up, preferred_element_type=jnp.float32))
    hidden_grad = part_sum(
        lax.dot_general(rows_c, q_down, contract_last, preferred_element_type=jnp.float32)
    )
    pre_wide = pre_b.astype(jnp.float32)
    hidden_b = jax.nn.silu(pre_wide).astype(jnp.bfloat16)
    pre_grad = (hidden_grad.astype(jnp.float32) * silu_grad(pre_wide)).astype(jnp.bfloat16)
    input_rows = lax.dot_general(
        pre_grad, q_up, contract_last, preferred_element_type=jnp.float32
    ).astype(jnp.bfloat16)
    g_up = lax.dot_general(
        rows_u, pre_grad, contract_first, preferred_element_type=jnp.float32
    ).astype(jnp.bfloat16)
    g_down = lax.dot_general(
        hidden_b, rows_c, contract_first, preferred_element_type=jnp.float32
    ).astype(jnp.bfloat16)
    input_rows, g_up, g_down = (input_rows.reshape(arrived_u.shape), g_up, g_down)
    returned_b = lax.all_to_all(input_rows, "expert", split_axis=0, concat_axis=0, tiled=True)
    (back_b,) = norm_back(unpack_rows(returned_b, disp_b, split_count))
    grad_in = (cot_b[0].astype(jnp.float32) + back_b).astype(jnp.bfloat16)
    next_a = passed_along(out_a, "pipe", 1)
    next_cot = passed_along(grad_in, "pipe", -1)
    dw_up, ds_up = quant_grads(w_up, s_up, g_up)
    dw_down, ds_down = quant_grads(w_down, s_down, g_down)
    up_sums, down_sums = lax.psum((is_mine * ds_up, is_mine * ds_down), "expert")
    return (
        next_a[None],
        next_cot[None],
        dw_up.astype(jnp.bfloat16)[None],
        dw_down.astype(jnp.bfloat16)[None],
        up_sums[None],
        down_sums[None],
    )


def solution(mesh):
    return jax.shard_map(
        shards,
        mesh=mesh,
        in_specs=(
            P("pipe", "expert", None),
            P("pipe", "expert", None),
            P("pipe", "expert", None),
            P("pipe", "expert", None),
            P("pipe", "expert", None),
            P("pipe", "expert", None),
            P("pipe", "expert", None),
            P("pipe", "expert", None),
            P("pipe", None, "expert"),
            P("pipe", None),
            P("pipe", None),
        ),
        out_specs=(
            P("pipe", "expert", None),
            P("pipe", "expert", None),
            P("pipe", "expert", None),
            P("pipe", None, "expert"),
            P("pipe", None),
            P("pipe", None),
        ),
        check_vma=False,
    )
```

profile of v0, /device:TPU:16, one launch (start us, length us, event | category | flops | bytes accessed | tf_op | source)
XLA Modules:
  0.0 673.8 jit_solution(16086297080142471165)
XLA Ops:
  8.6 11.4 %all-to-all-start.3 = ((bf16[32,34,896]{2,1,0:T(8,128)(2,1)}), bf16[32,34,896]{2,1,0:T(8,128)(2,1)S(1)}, u32[]{:S(2)}, u32[]{:S(2)}) async-start(bf16[32,34,896]{2,1,0:T(8,128)(2,1)} %copy.61), calls=%async_computation.3 | async-start | bytes 4587520 | tf_op jit(solution)/shard_map/all_to_all | solution.py:175
  24.2 52.0 %all-to-all-done.3 = bf16[32,34,896]{2,1,0:T(8,128)(2,1)S(1)} async-done(((bf16[32,34,896]{2,1,0:T(8,128)(2,1)}), bf16[32,34,896]{2,1,0:T(8,128)(2,1)S(1)}, u32[]{:S(2)}, u32[]{:S(2)}) %all-to-all-start.3) | async-done | bytes 1949728 | tf_op jit(solution)/shard_map/all_to_all | solution.py:175
  86.2 51.1 %all-to-all-done.2 = bf16[32,34,896]{2,1,0:T(8,128)(2,1)} async-done(((bf16[32,34,896]{2,1,0:T(8,128)(2,1)}), bf16[32,34,896]{2,1,0:T(8,128)(2,1)}, u32[]{:S(2)}, u32[]{:S(2)}) %all-to-all-start.2) | async-done | bytes 1949728 | tf_op jit(solution)/shard_map/all_to_all | solution.py:176
  137.3 5.0 all-to-all-start
  145.5 17.4 %fusion.128 = f32[1088,1024]{1,0:T(8,128)S(1)} fusion(bf16[1088,896]{1,0:T(8,128)(2,1)} %reshape.134, f32[]{:T(128)} %fusion.110, bf16[1,896,1024]{2,1,0:T(8,128)(2,1)} %param.18), kind=kOutput, calls=%fused_computation.229 | convolution fusion | flops 2003828736 | bytes 8241156 | tf_op jit(solution)/shard_map/dot_general | solution.py:180
  168.5 17.0 %fusion.44 = f32[1088,1024]{1,0:T(8,128)S(1)} fusion(bf16[1088,896]{1,0:T(8,128)(2,1)S(1)} %reshape.132, f32[]{:T(128)} %fusion.109, bf16[1,1024,896]{2,1,0:T(8,128)(2,1)} %param.19), kind=kOutput, calls=%fused_computation.86 | convolution fusion | flops 2003828736 | bytes 8241156 | tf_op jit(solution)/shard_map/dot_general | solution.py:182
  189.0 9.3 %all-to-all-done = bf16[32,34,896]{2,1,0:T(8,128)(2,1)} async-done(((bf16[32,34,896]{2,1,0:T(8,128)(2,1)}), bf16[32,34,896]{2,1,0:T(8,128)(2,1)}, u32[]{:S(2)}, u32[]{:S(2)}) %all-to-all-start) | async-done | bytes 1949728 | tf_op jit(solution)/shard_map/all_to_all | solution.py:156
  202.4 17.7 %fusion.130 = f32[1088,1024]{1,0:T(8,128)S(1)} fusion(bf16[1088,896]{1,0:T(8,128)(2,1)} %reshape.127, f32[]{:T(128)} %fusion.110, bf16[1,896,1024]{2,1,0:T(8,128)(2,1)} %param.18), kind=kOutput, calls=%fused_computation.230 | convolution fusion | flops 2003828736 | bytes 8241156 | tf_op jit(solution)/shard_map/dot_general | solution.py:160
  231.0 21.0 %collective-permute-done.14 = f32[1088,256]{1,0:T(8,128)S(1)} collective-permute-done((f32[1088,256]{1,0:T(8,128)S(1)}, f32[1088,256]{1,0:T(8,128)S(1)}, u32[]{:S(2)}, u32[]{:S(2)}) %collective-permute-start.14) | collective-permute-done | bytes 1114144 | tf_op jit(solution)/shard_map/ppermute | solution.py:21
  252.4 35.4 %collective-permute-done.8 = f32[1088,256]{1,0:T(8,128)S(1)} collective-permute-done((f32[1088,256]{1,0:T(8,128)S(1)}, f32[1088,256]{1,0:T(8,128)S(1)}, u32[]{:S(2)}, u32[]{:S(2)}) %collective-permute-start.8) | collective-permute-done | bytes 1114144 | tf_op jit(solution)/shard_map/ppermute | solution.py:21
  288.2 30.0 %collective-permute-done.1 = f32[1088,256]{1,0:T(8,128)S(1)} collective-permute-done((f32[1088,256]{1,0:T(8,128)S(1)}, f32[1088,256]{1,0:T(8,128)S(1)}, u32[]{:S(2)}, u32[]{:S(2)}) %collective-permute-start.1) | collective-permute-done | bytes 1114144 | tf_op jit(solution)/shard_map/ppermute | solution.py:21
  322.0 30.4 %collective-permute-done.9 = f32[1088,128]{1,0:T(8,128)S(1)} collective-permute-done((f32[1088,128]{1,0:T(8,128)S(1)}, f32[1088,128]{1,0:T(8,128)S(1)}, u32[]{:S(2)}, u32[]{:S(2)}) %collective-permute-start.9) | collective-permute-done | bytes 557088 | tf_op jit(solution)/shard_map/ppermute | solution.py:21
  352.6 17.7 %collective-permute-done.2 = f32[1088,128]{1,0:T(8,128)S(1)} collective-permute-done((f32[1088,128]{1,0:T(8,128)S(1)}, f32[1088,128]{1,0:T(8,128)S(1)}, u32[]{:S(2)}, u32[]{:S(2)}) %collective-permute-start.2) | collective-permute-done | bytes 557088 | tf_op jit(solution)/shard_map/ppermute | solution.py:21
  370.5 5.9 collective-permute-done.16
  376.5 5.8 collective-permute-done.10
  382.5 15.9 %collective-permute-done.17 = bf16[1088,256]{1,0:T(8,128)(2,1)S(1)} collective-permute-done((bf16[1088,256]{1,0:T(8,128)(2,1)S(1)}, bf16[1088,256]{1,0:T(8,128)(2,1)S(1)}, u32[]{:S(2)}, u32[]{:S(2)}) %collective-permute-start.17) | collective-permute-done | bytes 557088 | tf_op jit(solution)/shard_map/ppermute | solution.py:21
  398.8 11.4 %collective-permute-done.11 = bf16[1088,256]{1,0:T(8,128)(2,1)S(1)} collective-permute-done((bf16[1088,256]{1,0:T(8,128)(2,1)S(1)}, bf16[1088,256]{1,0:T(8,128)(2,1)S(1)}, u32[]{:S(2)}, u32[]{:S(2)}) %collective-permute-start.11) | collective-permute-done | bytes 557088 | tf_op jit(solution)/shard_map/ppermute | solution.py:21
  417.2 17.1 %convolution_convert_fusion = bf16[1088,896]{1,0:T(8,128)(2,1)S(1)} fusion(bf16[1088,1024]{1,0:T(8,128)(2,1)S(1)} %fusion.12, f32[]{:T(128)} %fusion.110, bf16[1,896,1024]{2,1,0:T(8,128)(2,1)S(1)} %copy-done.28), kind=kOutput, calls=%fused_computation.57 | convolution fusion | flops 2004803584 | bytes 6012932 | tf_op jit(solution)/shard_map/dot_general | solution.py:187
  449.2 17.0 %convolution_convert_fusion.1 = bf16[1088,896]{1,0:T(8,128)(2,1)} fusion(bf16[1088,512]{1,0:T(8,128)(2,1)S(1)} %get-tuple-element.17, bf16[1088,512]{1,0:T(8,128)(2,1)S(1)} %get-tuple-element.16, f32[]{:T(128)} %fusion.109, bf16[1,1024,896]{2,1,0:T(8,128)(2,1)S(1)} %copy-done.27), kind=kOutput, calls=%fused_computation.58 | convolution fusion | flops 2014830592 | bytes 6012932 | tf_op jit(solution)/shard_map/dot_general | solution.py:162
  470.2 26.5 %all-to-all-done.4 = bf16[32,34,896]{2,1,0:T(8,128)(2,1)S(1)} async-done(((bf16[32,34,896]{2,1,0:T(8,128)(2,1)}), bf16[32,34,896]{2,1,0:T(8,128)(2,1)S(1)}, u32[]{:S(2)}, u32[]{:S(2)}) %all-to-all-start.4) | async-done | bytes 1949728 | tf_op jit(solution)/shard_map/all_to_all | solution.py:197
  501.5 32.1 %fusion.17 = (f32[]{:T(128)}, bf16[1,1024,896]{2,1,0:T(8,128)(2,1)}) fusion(f32[]{:T(128)} %fusion.109, bf16[1,1024,896]{2,1,0:T(8,128)(2,1)} %param.19, bf16[1088,896]{1,0:T(8,128)(2,1)} %copy-done.15, bf16[1088,512]{1,0:T(8,128)(2,1)} %copy-done.7, bf16[1088,512]{1,0:T(8,128)(2,1)S(1)} %copy-done.6), kind=kOutput, calls=%fused_computation.28 | convolution fusion | flops 2024865792 | bytes 7847944 | tf_op jit(solution)/shard_map/dot_general | solution.py:193
  545.2 12.3 %all-to-all-done.1 = bf16[32,34,896]{2,1,0:T(8,128)(2,1)} async-done(((bf16[32,34,896]{2,1,0:T(8,128)(2,1)}), bf16[32,34,896]{2,1,0:T(8,128)(2,1)}, u32[]{:S(2)}, u32[]{:S(2)}) %all-to-all-start.1) | async-done | bytes 1949728 | tf_op jit(solution)/shard_map/all_to_all | solution.py:163
  569.3 33.8 %fusion.15 = (f32[]{:T(128)}, bf16[1,896,1024]{2,1,0:T(8,128)(2,1)}) fusion(f32[]{:T(128)} %fusion.110, bf16[1,896,1024]{2,1,0:T(8,128)(2,1)} %param.18, bf16[1088,896]{1,0:T(8,128)(2,1)S(1)} %copy-done.14, bf16[1088,1024]{1,0:T(8,128)(2,1)S(1)} %copy-done.13), kind=kOutput, calls=%fused_computation.26 | convolution fusion | flops 2014838784 | bytes 7847944 | tf_op jit(solution)/shard_map/dot_general | solution.py:190
  603.8 66.7 %all-reduce = (f32[1,4]{1,0:T(1,128)}, f32[1,4]{1,0:T(1,128)}) all-reduce(f32[1,4]{1,0:T(1,128)S(1)} %get-tuple-element.37, f32[1,4]{1,0:T(1,128)S(1)} %get-tuple-element.36), channel_id=1, replica_groups=mesh['pipe'=8,'expert'=32] {'expert'}, use_global_device_ids=true, to_apply=%region_10.11 | all-reduce | flops 8 | bytes 64 | tf_op jit(solution)/shard_map/psum | solution.py:204
  (199 shorter events, 110.8 us)
Async XLA Ops:
  8.6 67.6 %all-to-all-start.3 = ((bf16[32,34,896]{2,1,0:T(8,128)(2,1)}), bf16[32,34,896]{2,1,0:T(8,128)(2,1)S(1)}, u32[]{:S(2)}, u32[]{:S(2)}) async-start(bf16[32,34,896]{2,1,0:T(8,128)(2,1)} %copy.61), calls=%async_computation.3 | async-start | bytes 4587520 | tf_op jit(solution)/shard_map/all_to_all | solution.py:175
  76.2 61.0 %all-to-all-start.2 = ((bf16[32,34,896]{2,1,0:T(8,128)(2,1)}), bf16[32,34,896]{2,1,0:T(8,128)(2,1)}, u32[]{:S(2)}, u32[]{:S(2)}) async-start(bf16[32,34,896]{2,1,0:T(8,128)(2,1)} %bitcast.216), calls=%async_computation.2 | async-start | bytes 4587520 | tf_op jit(solution)/shard_map/all_to_all | solution.py:176
  137.3 61.1 %all-to-all-start = ((bf16[32,34,896]{2,1,0:T(8,128)(2,1)}), bf16[32,34,896]{2,1,0:T(8,128)(2,1)}, u32[]{:S(2)}, u32[]{:S(2)}) async-start(bf16[32,34,896]{2,1,0:T(8,128)(2,1)} %copy.51), calls=%async_computation | async-start | bytes 4587520 | tf_op jit(solution)/shard_map/all_to_all | solution.py:156
  165.6 55.1 %collective-permute-start.13 = (f32[1088,512]{1,0:T(8,128)}, f32[1088,512]{1,0:T(8,128)}, u32[]{:S(2)}, u32[]{:S(2)}) collective-permute-start(f32[1088,512]{1,0:T(8,128)} %slice_select_fusion), channel_id=1, source_target_pairs={{0,1},{1,0},{2,3},{3,2},{4,5},{5,4},{6,7},{7,6},{8,9},{9,8},{10,11... | collective-permute-start | bytes 6684680 | tf_op jit(solution)/shard_map/ppermute | solution.py:21
  188.4 38.2 %collective-permute-start.7 = (f32[1088,512]{1,0:T(8,128)}, f32[1088,512]{1,0:T(8,128)S(1)}, u32[]{:S(2)}, u32[]{:S(2)}) collective-permute-start(f32[1088,512]{1,0:T(8,128)} %slice_select_fusion.1), channel_id=1, source_target_pairs={{0,1},{1,0},{2,3},{3,2},{4,5},{5,4},{6,7},{7,6},{8,9},{9,8},{10,11... | collective-permute-start | bytes 6684680 | tf_op jit(solution)/shard_map/ppermute | solution.py:21
  220.6 7.3 %collective-permute-start = (f32[1088,512]{1,0:T(8,128)S(1)}, f32[1088,512]{1,0:T(8,128)S(1)}, u32[]{:S(2)}, u32[]{:S(2)}) collective-permute-start(f32[1088,512]{1,0:T(8,128)S(1)} %slice_select_fusion.2), channel_id=1, source_target_pairs={{0,1},{1,0},{2,3},{3,2},{4,5},{5,4},{6,7},{7,6},{8,9},{9,8},{10,11... | collective-permute-start | bytes 6684680 | tf_op jit(solution)/shard_map/ppermute | solution.py:21
  223.7 28.3 %collective-permute-start.14 = (f32[1088,256]{1,0:T(8,128)S(1)}, f32[1088,256]{1,0:T(8,128)S(1)}, u32[]{:S(2)}, u32[]{:S(2)}) collective-permute-start(f32[1088,256]{1,0:T(8,128)S(1)} %slice_select_fusion.3), channel_id=1, source_target_pairs={{0,2},{1,3},{2,0},{3,1},{4,6},{5,7},{6,4},{7,5},{8,10},{9,11},{10,... | collective-permute-start | bytes 3342344 | tf_op jit(solution)/shard_map/ppermute | solution.py:21
  227.6 60.2 %collective-permute-start.8 = (f32[1088,256]{1,0:T(8,128)S(1)}, f32[1088,256]{1,0:T(8,128)S(1)}, u32[]{:S(2)}, u32[]{:S(2)}) collective-permute-start(f32[1088,256]{1,0:T(8,128)S(1)} %slice_select_fusion.4), channel_id=1, source_target_pairs={{0,2},{1,3},{2,0},{3,1},{4,6},{5,7},{6,4},{7,5},{8,10},{9,11},{10,... | collective-permute-start | bytes 3342344 | tf_op jit(solution)/shard_map/ppermute | solution.py:21
  228.9 89.3 %collective-permute-start.1 = (f32[1088,256]{1,0:T(8,128)S(1)}, f32[1088,256]{1,0:T(8,128)S(1)}, u32[]{:S(2)}, u32[]{:S(2)}) collective-permute-start(f32[1088,256]{1,0:T(8,128)S(1)} %slice_select_fusion.5), channel_id=1, source_target_pairs={{0,2},{1,3},{2,0},{3,1},{4,6},{5,7},{6,4},{7,5},{8,10},{9,11},{10,... | collective-permute-start | bytes 3342344 | tf_op jit(solution)/shard_map/ppermute | solution.py:21
  252.3 69.5 %collective-permute-start.15 = (f32[1088,128]{1,0:T(8,128)S(1)}, f32[1088,128]{1,0:T(8,128)S(1)}, u32[]{:S(2)}, u32[]{:S(2)}) collective-permute-start(f32[1088,128]{1,0:T(8,128)S(1)} %slice_select_fusion.6), channel_id=1, source_target_pairs={{0,4},{1,5},{2,6},{3,7},{4,0},{5,1},{6,2},{7,3},{8,12},{9,13},{10,... | collective-permute-start | bytes 1671176 | tf_op jit(solution)/shard_map/ppermute | solution.py:21
  288.1 64.3 %collective-permute-start.9 = (f32[1088,128]{1,0:T(8,128)S(1)}, f32[1088,128]{1,0:T(8,128)S(1)}, u32[]{:S(2)}, u32[]{:S(2)}) collective-permute-start(f32[1088,128]{1,0:T(8,128)S(1)} %slice_select_fusion.7), channel_id=1, source_target_pairs={{0,4},{1,5},{2,6},{3,7},{4,0},{5,1},{6,2},{7,3},{8,12},{9,13},{10,... | collective-permute-start | bytes 1671176 | tf_op jit(solution)/shard_map/ppermute | solution.py:21
  318.5 51.8 %collective-permute-start.2 = (f32[1088,128]{1,0:T(8,128)S(1)}, f32[1088,128]{1,0:T(8,128)S(1)}, u32[]{:S(2)}, u32[]{:S(2)}) collective-permute-start(f32[1088,128]{1,0:T(8,128)S(1)} %slice_select_fusion.8), channel_id=1, source_target_pairs={{0,4},{1,5},{2,6},{3,7},{4,0},{5,1},{6,2},{7,3},{8,12},{9,13},{10,... | collective-permute-start | bytes 1671176 | tf_op jit(solution)/shard_map/ppermute | solution.py:21
  321.9 54.4 %collective-permute-start.16 = (bf16[1088,128]{1,0:T(8,128)(2,1)S(1)}, bf16[1088,128]{1,0:T(8,128)(2,1)S(1)}, u32[]{:S(2)}, u32[]{:S(2)}) collective-permute-start(bf16[1088,128]{1,0:T(8,128)(2,1)S(1)} %add_convert_fusion), channel_id=1, source_target_pairs={{0,4},{1,5},{2,6},{3,7},{4,0},{5,1},{6,2},{7,3},{8,12},{9,13},{10,... | collective-permute-start | bytes 835592 | tf_op jit(solution)/shard_map/ppermute | solution.py:21
  352.5 29.8 %collective-permute-start.10 = (bf16[1088,128]{1,0:T(8,128)(2,1)S(1)}, bf16[1088,128]{1,0:T(8,128)(2,1)S(1)}, u32[]{:S(2)}, u32[]{:S(2)}) collective-permute-start(bf16[1088,128]{1,0:T(8,128)(2,1)S(1)} %add_convert_fusion.1), channel_id=1, source_target_pairs={{0,4},{1,5},{2,6},{3,7},{4,0},{5,1},{6,2},{7,3},{8,12},{9,13},{10,... | collective-permute-start | bytes 835592 | tf_op jit(solution)/shard_map/ppermute | solution.py:21
  370.4 40.3 %collective-permute-start.3 = (bf16[1088,128]{1,0:T(8,128)(2,1)S(1)}, bf16[1088,128]{1,0:T(8,128)(2,1)S(1)}, u32[]{:S(2)}, u32[]{:S(2)}) collective-permute-start(bf16[1088,128]{1,0:T(8,128)(2,1)S(1)} %add_convert_fusion.2), channel_id=1, source_target_pairs={{0,4},{1,5},{2,6},{3,7},{4,0},{5,1},{6,2},{7,3},{8,12},{9,13},{10,... | collective-permute-start | bytes 835592 | tf_op jit(solution)/shard_map/ppermute | solution.py:21
  376.4 21.9 %collective-permute-start.17 = (bf16[1088,256]{1,0:T(8,128)(2,1)S(1)}, bf16[1088,256]{1,0:T(8,128)(2,1)S(1)}, u32[]{:S(2)}, u32[]{:S(2)}) collective-permute-start(bf16[1088,256]{1,0:T(8,128)(2,1)S(1)} %pad_maximum_fusion.7), channel_id=1, source_target_pairs={{0,2},{1,3},{2,0},{3,1},{4,6},{5,7},{6,4},{7,5},{8,10},{9,11},{10,... | collective-permute-start | bytes 1671176 | tf_op jit(solution)/shard_map/ppermute | solution.py:21
  382.4 27.8 %collective-permute-start.11 = (bf16[1088,256]{1,0:T(8,128)(2,1)S(1)}, bf16[1088,256]{1,0:T(8,128)(2,1)S(1)}, u32[]{:S(2)}, u32[]{:S(2)}) collective-permute-start(bf16[1088,256]{1,0:T(8,128)(2,1)S(1)} %pad_maximum_fusion.6), channel_id=1, source_target_pairs={{0,2},{1,3},{2,0},{3,1},{4,6},{5,7},{6,4},{7,5},{8,10},{9,11},{10,... | collective-permute-start | bytes 1671176 | tf_op jit(solution)/shard_map/ppermute | solution.py:21
  398.7 12.8 %collective-permute-start.18 = (bf16[1088,512]{1,0:T(8,128)(2,1)S(1)}, bf16[1088,512]{1,0:T(8,128)(2,1)S(1)}, u32[]{:S(2)}, u32[]{:S(2)}) collective-permute-start(bf16[1088,512]{1,0:T(8,128)(2,1)S(1)} %pad_maximum_fusion.4), channel_id=1, source_target_pairs={{0,1},{1,0},{2,3},{3,2},{4,5},{5,4},{6,7},{7,6},{8,9},{9,8},{10,11... | collective-permute-start | bytes 3342344 | tf_op jit(solution)/shard_map/ppermute | solution.py:21
  410.8 29.7 %collective-permute-start.4 = (bf16[1088,256]{1,0:T(8,128)(2,1)S(1)}, bf16[1088,256]{1,0:T(8,128)(2,1)}, u32[]{:S(2)}, u32[]{:S(2)}) collective-permute-start(bf16[1088,256]{1,0:T(8,128)(2,1)S(1)} %pad_maximum_fusion.5), channel_id=1, source_target_pairs={{0,2},{1,3},{2,0},{3,1},{4,6},{5,7},{6,4},{7,5},{8,10},{9,11},{10,... | collective-permute-start | bytes 1671176 | tf_op jit(solution)/shard_map/ppermute | solution.py:21
  436.5 60.2 %all-to-all-start.4 = ((bf16[32,34,896]{2,1,0:T(8,128)(2,1)}), bf16[32,34,896]{2,1,0:T(8,128)(2,1)S(1)}, u32[]{:S(2)}, u32[]{:S(2)}) async-start(bf16[32,34,896]{2,1,0:T(8,128)(2,1)} %reshape.135), calls=%async_computation.4 | async-start | bytes 4587520 | tf_op jit(solution)/shard_map/all_to_all | solution.py:197
  443.1 4.3 collective-permute-start.5
  496.6 60.9 %all-to-all-start.1 = ((bf16[32,34,896]{2,1,0:T(8,128)(2,1)}), bf16[32,34,896]{2,1,0:T(8,128)(2,1)}, u32[]{:S(2)}, u32[]{:S(2)}) async-start(bf16[32,34,896]{2,1,0:T(8,128)(2,1)} %reshape.128), calls=%async_computation.1 | async-start | bytes 4587520 | tf_op jit(solution)/shard_map/all_to_all | solution.py:163
  542.6 127.9 %collective-permute-start.19 = (bf16[64,7168]{1,0:T(8,128)(2,1)}, bf16[64,7168]{1,0:T(8,128)(2,1)}, u32[]{:S(2)}, u32[]{:S(2)}) collective-permute-start(bf16[64,7168]{1,0:T(8,128)(2,1)} %fusion.41), channel_id=1, source_target_pairs={{32,0},{64,32},{96,64},{128,96},{160,128},{192,160},{224,192},{33,... | collective-permute-start | bytes 2752520 | tf_op jit(solution)/shard_map/ppermute | solution.py:27
  566.8 103.7 %collective-permute-start.6 = (bf16[64,7168]{1,0:T(8,128)(2,1)}, bf16[64,7168]{1,0:T(8,128)(2,1)S(1)}, u32[]{:S(2)}, u32[]{:S(2)}) collective-permute-start(bf16[64,7168]{1,0:T(8,128)(2,1)} %fusion.1), channel_id=1, source_target_pairs={{0,32},{32,64},{64,96},{96,128},{128,160},{160,192},{192,224},{1,3... | collective-permute-start | bytes 2752520 | tf_op jit(solution)/shard_map/ppermute | solution.py:27
  (36 other events, 387.2 us)
where the time goes:
time: 682 us; the launch traced here: 674 us
  waiting for transfers between devices  326 us (48%)
  matrix products  164 us (24%)
  blocking collectives  66.7 us (10%)
  starting transfers between devices  46.4 us (7%)
  local copies, waits for them, and re-layouts  43 us (6%)
  other arithmetic  25 us (4%)
    ppermute x18, waiting for transfers between devices, partner_2(): lax.ppermute(value, axis, [(i, i ^ 1 << bit) for i in range(lax.axis_size...  175 us
    psum x1, blocking collectives, shards(): lax.psum((is_mine * ds_up, is_mine * ds_down), 'expert')  66.7 us
    all_to_all x1, waiting for transfers between devices, shards(): lax.all_to_all(send_u, 'expert', split_axis=0, concat_axis=0, tiled=True)  52 us
    all_to_all x1, waiting for transfers between devices, shards(): lax.all_to_all(send_c, 'expert', split_axis=0, concat_axis=0, tiled=True)  51.1 us
    dot_general x1, matrix products, shards(): lax.dot_general(rows_u, pre_grad, contract_first, preferred_element_type=...  33.8 us
    dot_general x1, matrix products, shards(): lax.dot_general(hidden_b, rows_c, contract_first, preferred_element_type=...  32.1 us
    all_to_all x1, waiting for transfers between devices, shards(): lax.all_to_all(input_rows, 'expert', split_axis=0, concat_axis=0, tiled=T...  26.5 us
    dot_general x1, matrix products, shards(): pre_a = part_sum(jnp.dot(rows_in, q_up, preferred_element_type=jnp.float32))  17.7 us
  transfers between devices with their start and end apart: 25, of which 15 were waited for; matrix products, arithmetic and copies ran while one was open for 32% of the time, Pallas kernels for 0%

commit v1 on v0

--- a/solution.py
+++ b/solution.py
@@ -31,24 +31,46 @@
     return values * lax.rsqrt(jnp.mean(values * values, axis=-1, keepdims=True) + epsilon)
 
 
-def soft_round(values):
-    return values - jnp.sin(two_pi * values) / two_pi
-
-
-def fake_quant(weights, scale):
-    ratio = weights.astype(jnp.float32) / scale
-    return scale * soft_round(jnp.clip(ratio, -qlimit, qlimit))
-
-
-def quant_grads(weights, scale, grads):
-    ratio = weights.astype(jnp.float32) / scale
+SIN_PI = (3.1415927410125732, -5.167710304260254, 2.550077438354492, -0.598291277885437, 0.07765766233205795)
+COS_PI = (
+    1.0,
+    -4.934802055358887,
+    4.058709144592285,
+    -1.335211992263794,
+    0.23493731021881104,
+    -0.024396324530243874,
+)
+
+
+def poly(coefs, square):
+    total = coefs[-1]
+    for coef in coefs[-2::-1]:
+        total = total * square + coef
+    return total
+
+
+def half_waves(values):
+    rest = values - jnp.round(values)
+    square = rest * rest
+    return (rest * poly(SIN_PI, square), poly(COS_PI, square))
+
+
+def fake_quant(weights, inverse, scale):
+    ratio = jnp.clip(weights.astype(jnp.float32) * inverse, -qlimit, qlimit)
+    sine, cosine = half_waves(ratio)
+    return scale * (ratio - sine * cosine * (1.0 / math.pi))
+
+
+def quant_grads(weights, inverse, grads):
+    ratio = weights.astype(jnp.float32) * inverse
     inside = jnp.abs(ratio) < qlimit
-    wave = 1.0 - jnp.cos(two_pi * ratio)
+    clipped = jnp.clip(ratio, -qlimit, qlimit)
+    sine, cosine = half_waves(clipped)
+    wave = jnp.where(inside, 2.0 * sine * sine, 0.0)
     grads_wide = grads.astype(jnp.float32)
-    weight_grad = grads_wide * jnp.where(inside, wave, 0.0)
-    slope = soft_round(jnp.clip(ratio, -qlimit, qlimit)) - jnp.where(inside, ratio * wave, 0.0)
+    slope = clipped - sine * cosine * (1.0 / math.pi) - clipped * wave
     scale_grad = jnp.sum(grads_wide * slope) / math.sqrt(D * HID * qlimit)
-    return (weight_grad, scale_grad)
+    return (grads_wide * wave, scale_grad)
 
 
 def silu_grad(values):
@@ -61,7 +83,9 @@
     entries = flat_ids.shape[0]
     chosen = routes.shape[1]
     matches = (flat_ids[:, None] == jnp.arange(EXPERTS, dtype=jnp.int32)[None, :]).astype(jnp.int32)
-    before = jnp.cumsum(matches, axis=0) - matches
+    order = jnp.arange(entries, dtype=jnp.int32)
+    earlier = (order[:, None] > order[None, :]).astype(jnp.float32)
+    before = jnp.dot(earlier, matches.astype(jnp.float32), precision=highest).astype(jnp.int32)
     slot_of = jnp.sum(before * matches, axis=1)
     at_slot = (slot_of[:, None] == jnp.arange(CAP, dtype=jnp.int32)[None, :]).astype(jnp.float32)
     owner_of = (
@@ -123,8 +147,14 @@
     s_down = jnp.sum(is_mine * down_scale[0])
     w_up = up_weight[0]
     w_down = down_weight[0]
-    q_up = fake_quant(w_up, s_up).astype(jnp.bfloat16)
-    q_down = fake_quant(w_down, s_down).astype(jnp.bfloat16)
+    inv_up = 1.0 / s_up
+    inv_down = 1.0 / s_down
+    q_up, q_down = lax.optimization_barrier(
+        (
+            fake_quant(w_up, inv_up, s_up).astype(jnp.bfloat16),
+            fake_quant(w_down, inv_down, s_down).astype(jnp.bfloat16),
+        )
+    )
     part_width = w_up.shape[0]
     contract_last = (((1,), (1,)), ((), ()))
     contract_first = (((0,), (0,)), ((), ()))
@@ -139,7 +169,8 @@
             upper_part = current[:, half_cols:]
             keep_part = jnp.where(upper_side, upper_part, lower_part)
             give_part = jnp.where(upper_side, lower_part, upper_part)
-            current = keep_part + partner_2(give_part, "expert", bit_no)
+            given = partner_2(give_part.astype(jnp.bfloat16), "expert", bit_no)
+            current = keep_part + given.astype(jnp.float32)
         current = current.astype(jnp.bfloat16)
         for bit_no in reversed(bit_order):
             partner = partner_2(current, "expert", bit_no)
@@ -199,9 +230,12 @@
     grad_in = (cot_b[0].astype(jnp.float32) + back_b).astype(jnp.bfloat16)
     next_a = passed_along(out_a, "pipe", 1)
     next_cot = passed_along(grad_in, "pipe", -1)
-    dw_up, ds_up = quant_grads(w_up, s_up, g_up)
-    dw_down, ds_down = quant_grads(w_down, s_down, g_down)
-    up_sums, down_sums = lax.psum((is_mine * ds_up, is_mine * ds_down), "expert")
+    dw_up, ds_up = quant_grads(w_up, inv_up, g_up)
+    dw_down, ds_down = quant_grads(w_down, inv_down, g_down)
+    sums = jnp.concatenate((is_mine * ds_up, is_mine * ds_down))
+    for bit_no in range(lax.axis_size("expert").bit_length() - 1):
+        sums = sums + partner_2(sums, "expert", bit_no)
+    up_sums, down_sums = (sums[:EXPERTS], sums[EXPERTS:])
     return (
         next_a[None],
         next_cot[None],

time: 682 us -> 531 us (0.78)
  matrix products: 164 us -> 51.3 us
  blocking collectives: 66.7 us -> 0 us
  waiting for transfers between devices: 326 us -> 337 us
    psum x1 -> x0, blocking collectives: 66.7 us -> none  [shards(): lax.psum((is_mine * ds_up, is_mine * ds_down), 'expert')]
    all_to_all x1, waiting for transfers between devices: 9.34 us -> 49.4 us  [shards(): lax.all_to_all(pack_rows(normed_a, disp_a, split_count), 'expert', split_...]
    ppermute x18 -> x23, waiting for transfers between devices: 175 us -> 141 us  [partner_2(): lax.ppermute(value, axis, [(i, i ^ 1 << bit) for i in range(lax.axis_size...]
    all_to_all x1, waiting for transfers between devices: 52 us -> 22.3 us  [shards(): lax.all_to_all(send_u, 'expert', split_axis=0, concat_axis=0, tiled=True)]
    all_to_all x1, waiting for transfers between devices: 12.3 us -> 39.2 us  [shards(): lax.all_to_all(outputs.reshape(arrived_a.shape), 'expert', split_axis=0,...]
    dot_general x1, matrix products: 33.8 us -> 8.42 us  [shards(): lax.dot_general(rows_u, pre_grad, contract_first, preferred_element_type=...]
    dot_general x1, matrix products: 32.1 us -> 11 us  [shards(): lax.dot_general(hidden_b, rows_c, contract_first, preferred_element_type=...]
    dot_general x1, matrix products: 17 us -> 2.53 us  [shards(): jnp.dot(hidden_a, q_down, preferred_element_type=jnp.float32)]
  transfers between devices with their start and end apart: 25 -> 30, of which waited for: 15 -> 22; matrix products, arithmetic and copies ran while one was open for 32% -> 22% of each run, Pallas kernels for 0% -> 0%
where the time goes in v1:
time: 531 us; the launch traced here: 523 us
  waiting for transfers between devices  337 us (63%)
  matrix products  51.3 us (10%)
  starting transfers between devices  50.5 us (10%)
  local copies, waits for them, and re-layouts  47.8 us (9%)
  other arithmetic  31.8 us (6%)
    ppermute x23, waiting for transfers between devices, partner_2(): lax.ppermute(value, axis, [(i, i ^ 1 << bit) for i in range(lax.axis_size...  141 us
    all_to_all x1, waiting for transfers between devices, shards(): lax.all_to_all(send_c, 'expert', split_axis=0, concat_axis=0, tiled=True)  51.5 us
    all_to_all x1, waiting for transfers between devices, shards(): lax.all_to_all(pack_rows(normed_a, disp_a, split_count), 'expert', split_...  49.4 us
    all_to_all x1, waiting for transfers between devices, shards(): lax.all_to_all(outputs.reshape(arrived_a.shape), 'expert', split_axis=0,...  39.2 us
    all_to_all x1, waiting for transfers between devices, shards(): lax.all_to_all(input_rows, 'expert', split_axis=0, concat_axis=0, tiled=T...  33.5 us
    all_to_all x1, waiting for transfers between devices, shards(): lax.all_to_all(send_u, 'expert', split_axis=0, concat_axis=0, tiled=True)  22.3 us
    ppermute x23, starting transfers between devices, partner_2(): lax.ppermute(value, axis, [(i, i ^ 1 << bit) for i in range(lax.axis_size...  15 us
    unnamed x67, local copies, waits for them, and re-layouts  14.9 us
  transfers between devices with their start and end apart: 30, of which 22 were waited for; matrix products, arithmetic and copies ran while one was open for 22% of the time, Pallas kernels for 0%

profile of v1, /device:TPU:16, one launch (start us, length us, event | category | flops | bytes accessed | tf_op | source)
XLA Modules:
  0.0 523.0 jit_solution(12668265449696608765)
XLA Ops:
  7.6 11.4 %all-to-all-start.2 = ((bf16[32,34,896]{2,1,0:T(8,128)(2,1)}), bf16[32,34,896]{2,1,0:T(8,128)(2,1)S(1)}, u32[]{:S(2)}, u32[]{:S(2)}) async-start(bf16[32,34,896]{2,1,0:T(8,128)(2,1)} %bitcast.230), calls=%async_computation.2 | async-start | bytes 4587520 | tf_op jit(solution)/shard_map/all_to_all | solution.py:207
  23.7 51.5 %all-to-all-done.2 = bf16[32,34,896]{2,1,0:T(8,128)(2,1)S(1)} async-done(((bf16[32,34,896]{2,1,0:T(8,128)(2,1)}), bf16[32,34,896]{2,1,0:T(8,128)(2,1)S(1)}, u32[]{:S(2)}, u32[]{:S(2)}) %all-to-all-start.2) | async-done | bytes 1949728 | tf_op jit(solution)/shard_map/all_to_all | solution.py:207
  75.1 4.8 all-to-all-start
  86.7 49.4 %all-to-all-done = bf16[32,34,896]{2,1,0:T(8,128)(2,1)} async-done(((bf16[32,34,896]{2,1,0:T(8,128)(2,1)}), bf16[32,34,896]{2,1,0:T(8,128)(2,1)}, u32[]{:S(2)}, u32[]{:S(2)}) %all-to-all-start) | async-done | bytes 1949728 | tf_op jit(solution)/shard_map/all_to_all | solution.py:187
  136.0 5.0 all-to-all-start.3
  141.0 6.4 %multiply_convert_fusion.1 = bf16[896,1024]{1,0:T(8,128)(2,1)} fusion(f32[]{:T(128)} %fusion.95, f32[]{:T(128)S(6)} %div.62, bf16[1,896,1024]{2,1,0:T(8,128)(2,1)} %param.18), kind=kLoop, calls=%fused_computation.51 | loop fusion | flops 27525120 | bytes 3670024 | tf_op jit(solution)/shard_map/convert_element_type | solution.py:154
  147.4 5.1 multiply_convert_fusion
  174.8 22.3 %all-to-all-done.3 = bf16[32,34,896]{2,1,0:T(8,128)(2,1)} async-done(((bf16[32,34,896]{2,1,0:T(8,128)(2,1)}), bf16[32,34,896]{2,1,0:T(8,128)(2,1)}, u32[]{:S(2)}, u32[]{:S(2)}) %all-to-all-start.3) | async-done | bytes 1949728 | tf_op jit(solution)/shard_map/all_to_all | solution.py:206
  215.3 8.4 %collective-permute-done.1 = bf16[1088,256]{1,0:T(8,128)(2,1)S(1)} collective-permute-done((bf16[1088,256]{1,0:T(8,128)(2,1)S(1)}, bf16[1088,256]{1,0:T(8,128)(2,1)S(1)}, u32[]{:S(2)}, u32[]{:S(2)}) %collective-permute-start.1) | collective-permute-done | bytes 557088 | tf_op jit(solution)/shard_map/ppermute | solution.py:21
  224.1 17.6 %collective-permute-done.8 = bf16[1088,256]{1,0:T(8,128)(2,1)S(1)} collective-permute-done((bf16[1088,256]{1,0:T(8,128)(2,1)S(1)}, bf16[1088,256]{1,0:T(8,128)(2,1)S(1)}, u32[]{:S(2)}, u32[]{:S(2)}) %collective-permute-start.8) | collective-permute-done | bytes 557088 | tf_op jit(solution)/shard_map/ppermute | solution.py:21
  242.0 12.2 %collective-permute-done.14 = bf16[1088,256]{1,0:T(8,128)(2,1)S(1)} collective-permute-done((bf16[1088,256]{1,0:T(8,128)(2,1)S(1)}, bf16[1088,256]{1,0:T(8,128)(2,1)S(1)}, u32[]{:S(2)}, u32[]{:S(2)}) %collective-permute-start.14) | collective-permute-done | bytes 557088 | tf_op jit(solution)/shard_map/ppermute | solution.py:21
  257.9 23.7 %collective-permute-done.9 = bf16[1088,128]{1,0:T(8,128)(2,1)S(1)} collective-permute-done((bf16[1088,128]{1,0:T(8,128)(2,1)S(1)}, bf16[1088,128]{1,0:T(8,128)(2,1)S(1)}, u32[]{:S(2)}, u32[]{:S(2)}) %collective-permute-start.9) | collective-permute-done | bytes 278560 | tf_op jit(solution)/shard_map/ppermute | solution.py:21
  281.9 11.7 %collective-permute-done.15 = bf16[1088,128]{1,0:T(8,128)(2,1)S(1)} collective-permute-done((bf16[1088,128]{1,0:T(8,128)(2,1)S(1)}, bf16[1088,128]{1,0:T(8,128)(2,1)S(1)}, u32[]{:S(2)}, u32[]{:S(2)}) %collective-permute-start.15) | collective-permute-done | bytes 278560 | tf_op jit(solution)/shard_map/ppermute | solution.py:21
  293.8 5.8 %collective-permute-done.3 = bf16[1088,128]{1,0:T(8,128)(2,1)S(1)} collective-permute-done((bf16[1088,128]{1,0:T(8,128)(2,1)S(1)}, bf16[1088,128]{1,0:T(8,128)(2,1)S(1)}, u32[]{:S(2)}, u32[]{:S(2)}) %collective-permute-start.3) | collective-permute-done | bytes 278560 | tf_op jit(solution)/shard_map/ppermute | solution.py:21
  299.8 5.9 %collective-permute-done.10 = bf16[1088,128]{1,0:T(8,128)(2,1)S(1)} collective-permute-done((bf16[1088,128]{1,0:T(8,128)(2,1)S(1)}, bf16[1088,128]{1,0:T(8,128)(2,1)S(1)}, u32[]{:S(2)}, u32[]{:S(2)}) %collective-permute-start.10) | collective-permute-done | bytes 278560 | tf_op jit(solution)/shard_map/ppermute | solution.py:21
  310.7 11.7 %collective-permute-done.4 = bf16[1088,256]{1,0:T(8,128)(2,1)S(1)} collective-permute-done((bf16[1088,256]{1,0:T(8,128)(2,1)S(1)}, bf16[1088,256]{1,0:T(8,128)(2,1)S(1)}, u32[]{:S(2)}, u32[]{:S(2)}) %collective-permute-start.4) | collective-permute-done | bytes 557088 | tf_op jit(solution)/shard_map/ppermute | solution.py:21
  322.8 11.5 %collective-permute-done.11 = bf16[1088,256]{1,0:T(8,128)(2,1)S(1)} collective-permute-done((bf16[1088,256]{1,0:T(8,128)(2,1)S(1)}, bf16[1088,256]{1,0:T(8,128)(2,1)S(1)}, u32[]{:S(2)}, u32[]{:S(2)}) %collective-permute-start.11) | collective-permute-done | bytes 557088 | tf_op jit(solution)/shard_map/ppermute | solution.py:21
  336.9 9.3 %collective-permute-done.17 = bf16[1088,256]{1,0:T(8,128)(2,1)S(1)} collective-permute-done((bf16[1088,256]{1,0:T(8,128)(2,1)S(1)}, bf16[1088,256]{1,0:T(8,128)(2,1)S(1)}, u32[]{:S(2)}, u32[]{:S(2)}) %collective-permute-start.17) | collective-permute-done | bytes 557088 | tf_op jit(solution)/shard_map/ppermute | solution.py:21
  374.7 39.2 %all-to-all-done.1 = bf16[32,34,896]{2,1,0:T(8,128)(2,1)S(1)} async-done(((bf16[32,34,896]{2,1,0:T(8,128)(2,1)}), bf16[32,34,896]{2,1,0:T(8,128)(2,1)S(1)}, u32[]{:S(2)}, u32[]{:S(2)}) %all-to-all-start.1) | async-done | bytes 1949728 | tf_op jit(solution)/shard_map/all_to_all | solution.py:194
  413.8 5.0 all-to-all-start.4
  419.3 11.0 %fusion.17 = (f32[]{:T(128)}, bf16[1,1024,896]{2,1,0:T(8,128)(2,1)}) fusion(bf16[1,1024,896]{2,1,0:T(8,128)(2,1)} %param.19, f32[]{:T(128)S(6)} %div.63, bf16[1088,896]{1,0:T(8,128)(2,1)} %reshape.141, bf16[1088,512]{1,0:T(8,128)(2,1)} %copy-done.11, bf16[1088,512]{1,0:T(8,128)(2,1)} %copy-done.10), kind=kOutput, calls=%fused_computation.32 | convolution fusion | flops 2044133376 | bytes 7847944 | tf_op jit(solution)/shard_map/dot_general | solution.py:224
  441.4 33.5 %all-to-all-done.4 = bf16[32,34,896]{2,1,0:T(8,128)(2,1)} async-done(((bf16[32,34,896]{2,1,0:T(8,128)(2,1)}), bf16[32,34,896]{2,1,0:T(8,128)(2,1)}, u32[]{:S(2)}, u32[]{:S(2)}) %all-to-all-start.4) | async-done | bytes 1949728 | tf_op jit(solution)/shard_map/all_to_all | solution.py:228
  486.8 8.4 %fusion.15 = (f32[]{:T(128)}, bf16[1,896,1024]{2,1,0:T(8,128)(2,1)}) fusion(bf16[1,896,1024]{2,1,0:T(8,128)(2,1)S(1)} %copy-done.18, f32[]{:T(128)S(6)} %div.62, bf16[1088,896]{1,0:T(8,128)(2,1)S(1)} %copy-done.16, bf16[1088,1024]{1,0:T(8,128)(2,1)S(1)} %copy-done.14), kind=kOutput, calls=%fused_computation.30 | convolution fusion | flops 2034106368 | bytes 7847944 | tf_op jit(solution)/shard_map/dot_general | solution.py:221
  506.9 7.2 %collective-permute-done.23 = f32[8]{0:T(128)S(1)} collective-permute-done((f32[8]{0:T(128)S(1)}, f32[8]{0:T(128)S(1)}, u32[]{:S(2)}, u32[]{:S(2)}) %collective-permute-start.23) | collective-permute-done | bytes 64 | tf_op jit(solution)/shard_map/ppermute | solution.py:21
  (199 shorter events, 140.8 us)
Async XLA Ops:
  7.6 67.6 %all-to-all-start.2 = ((bf16[32,34,896]{2,1,0:T(8,128)(2,1)}), bf16[32,34,896]{2,1,0:T(8,128)(2,1)S(1)}, u32[]{:S(2)}, u32[]{:S(2)}) async-start(bf16[32,34,896]{2,1,0:T(8,128)(2,1)} %bitcast.230), calls=%async_computation.2 | async-start | bytes 4587520 | tf_op jit(solution)/shard_map/all_to_all | solution.py:207
  75.1 60.9 %all-to-all-start = ((bf16[32,34,896]{2,1,0:T(8,128)(2,1)}), bf16[32,34,896]{2,1,0:T(8,128)(2,1)}, u32[]{:S(2)}, u32[]{:S(2)}) async-start(bf16[32,34,896]{2,1,0:T(8,128)(2,1)} %copy.49), calls=%async_computation | async-start | bytes 4587520 | tf_op jit(solution)/shard_map/all_to_all | solution.py:187
  136.0 61.1 %all-to-all-start.3 = ((bf16[32,34,896]{2,1,0:T(8,128)(2,1)}), bf16[32,34,896]{2,1,0:T(8,128)(2,1)}, u32[]{:S(2)}, u32[]{:S(2)}) async-start(bf16[32,34,896]{2,1,0:T(8,128)(2,1)} %copy.57), calls=%async_computation.3 | async-start | bytes 4587520 | tf_op jit(solution)/shard_map/all_to_all | solution.py:206
  164.4 40.7 %collective-permute-start = (bf16[1088,512]{1,0:T(8,128)(2,1)}, bf16[1088,512]{1,0:T(8,128)(2,1)}, u32[]{:S(2)}, u32[]{:S(2)}) collective-permute-start(bf16[1088,512]{1,0:T(8,128)(2,1)} %select_convert_fusion.2), channel_id=1, source_target_pairs={{0,1},{1,0},{2,3},{3,2},{4,5},{5,4},{6,7},{7,6},{8,9},{9,8},{10,11... | collective-permute-start | bytes 3342344 | tf_op jit(solution)/shard_map/ppermute | solution.py:21
  174.6 35.7 %collective-permute-start.7 = (bf16[1088,512]{1,0:T(8,128)(2,1)}, bf16[1088,512]{1,0:T(8,128)(2,1)}, u32[]{:S(2)}, u32[]{:S(2)}) collective-permute-start(bf16[1088,512]{1,0:T(8,128)(2,1)} %select_convert_fusion.1), channel_id=1, source_target_pairs={{0,1},{1,0},{2,3},{3,2},{4,5},{5,4},{6,7},{7,6},{8,9},{9,8},{10,11... | collective-permute-start | bytes 3342344 | tf_op jit(solution)/shard_map/ppermute | solution.py:21
  204.8 7.7 %collective-permute-start.13 = (bf16[1088,512]{1,0:T(8,128)(2,1)S(1)}, bf16[1088,512]{1,0:T(8,128)(2,1)S(1)}, u32[]{:S(2)}, u32[]{:S(2)}) collective-permute-start(bf16[1088,512]{1,0:T(8,128)(2,1)S(1)} %select_convert_fusion), channel_id=1, source_target_pairs={{0,1},{1,0},{2,3},{3,2},{4,5},{5,4},{6,7},{7,6},{8,9},{9,8},{10,11... | collective-permute-start | bytes 3342344 | tf_op jit(solution)/shard_map/ppermute | solution.py:21
  207.4 16.3 %collective-permute-start.1 = (bf16[1088,256]{1,0:T(8,128)(2,1)S(1)}, bf16[1088,256]{1,0:T(8,128)(2,1)S(1)}, u32[]{:S(2)}, u32[]{:S(2)}) collective-permute-start(bf16[1088,256]{1,0:T(8,128)(2,1)S(1)} %select_convert_fusion.5), channel_id=1, source_target_pairs={{0,2},{1,3},{2,0},{3,1},{4,6},{5,7},{6,4},{7,5},{8,10},{9,11},{10,... | collective-permute-start | bytes 1671176 | tf_op jit(solution)/shard_map/ppermute | solution.py:21
  212.4 29.2 %collective-permute-start.8 = (bf16[1088,256]{1,0:T(8,128)(2,1)S(1)}, bf16[1088,256]{1,0:T(8,128)(2,1)S(1)}, u32[]{:S(2)}, u32[]{:S(2)}) collective-permute-start(bf16[1088,256]{1,0:T(8,128)(2,1)S(1)} %select_convert_fusion.4), channel_id=1, source_target_pairs={{0,2},{1,3},{2,0},{3,1},{4,6},{5,7},{6,4},{7,5},{8,10},{9,11},{10,... | collective-permute-start | bytes 1671176 | tf_op jit(solution)/shard_map/ppermute | solution.py:21
  213.2 40.9 %collective-permute-start.14 = (bf16[1088,256]{1,0:T(8,128)(2,1)S(1)}, bf16[1088,256]{1,0:T(8,128)(2,1)S(1)}, u32[]{:S(2)}, u32[]{:S(2)}) collective-permute-start(bf16[1088,256]{1,0:T(8,128)(2,1)S(1)} %select_convert_fusion.3), channel_id=1, source_target_pairs={{0,2},{1,3},{2,0},{3,1},{4,6},{5,7},{6,4},{7,5},{8,10},{9,11},{10,... | collective-permute-start | bytes 1671176 | tf_op jit(solution)/shard_map/ppermute | solution.py:21
  224.0 33.8 %collective-permute-start.2 = (bf16[1088,128]{1,0:T(8,128)(2,1)S(1)}, bf16[1088,128]{1,0:T(8,128)(2,1)S(1)}, u32[]{:S(2)}, u32[]{:S(2)}) collective-permute-start(bf16[1088,128]{1,0:T(8,128)(2,1)S(1)} %select_convert_fusion.8), channel_id=1, source_target_pairs={{0,4},{1,5},{2,6},{3,7},{4,0},{5,1},{6,2},{7,3},{8,12},{9,13},{10,... | collective-permute-start | bytes 835592 | tf_op jit(solution)/shard_map/ppermute | solution.py:21
  241.9 39.8 %collective-permute-start.9 = (bf16[1088,128]{1,0:T(8,128)(2,1)S(1)}, bf16[1088,128]{1,0:T(8,128)(2,1)S(1)}, u32[]{:S(2)}, u32[]{:S(2)}) collective-permute-start(bf16[1088,128]{1,0:T(8,128)(2,1)S(1)} %select_convert_fusion.7), channel_id=1, source_target_pairs={{0,4},{1,5},{2,6},{3,7},{4,0},{5,1},{6,2},{7,3},{8,12},{9,13},{10,... | collective-permute-start | bytes 835592 | tf_op jit(solution)/shard_map/ppermute | solution.py:21
  254.4 39.1 %collective-permute-start.15 = (bf16[1088,128]{1,0:T(8,128)(2,1)S(1)}, bf16[1088,128]{1,0:T(8,128)(2,1)S(1)}, u32[]{:S(2)}, u32[]{:S(2)}) collective-permute-start(bf16[1088,128]{1,0:T(8,128)(2,1)S(1)} %select_convert_fusion.6), channel_id=1, source_target_pairs={{0,4},{1,5},{2,6},{3,7},{4,0},{5,1},{6,2},{7,3},{8,12},{9,13},{10,... | collective-permute-start | bytes 835592 | tf_op jit(solution)/shard_map/ppermute | solution.py:21
  257.8 41.7 %collective-permute-start.3 = (bf16[1088,128]{1,0:T(8,128)(2,1)S(1)}, bf16[1088,128]{1,0:T(8,128)(2,1)S(1)}, u32[]{:S(2)}, u32[]{:S(2)}) collective-permute-start(bf16[1088,128]{1,0:T(8,128)(2,1)S(1)} %add_convert_fusion.2), channel_id=1, source_target_pairs={{0,4},{1,5},{2,6},{3,7},{4,0},{5,1},{6,2},{7,3},{8,12},{9,13},{10,... | collective-permute-start | bytes 835592 | tf_op jit(solution)/shard_map/ppermute | solution.py:21
  281.8 23.9 %collective-permute-start.10 = (bf16[1088,128]{1,0:T(8,128)(2,1)S(1)}, bf16[1088,128]{1,0:T(8,128)(2,1)S(1)}, u32[]{:S(2)}, u32[]{:S(2)}) collective-permute-start(bf16[1088,128]{1,0:T(8,128)(2,1)S(1)} %add_convert_fusion.1), channel_id=1, source_target_pairs={{0,4},{1,5},{2,6},{3,7},{4,0},{5,1},{6,2},{7,3},{8,12},{9,13},{10,... | collective-permute-start | bytes 835592 | tf_op jit(solution)/shard_map/ppermute | solution.py:21
  293.7 16.8 %collective-permute-start.16 = (bf16[1088,128]{1,0:T(8,128)(2,1)S(1)}, bf16[1088,128]{1,0:T(8,128)(2,1)S(1)}, u32[]{:S(2)}, u32[]{:S(2)}) collective-permute-start(bf16[1088,128]{1,0:T(8,128)(2,1)S(1)} %add_convert_fusion), channel_id=1, source_target_pairs={{0,4},{1,5},{2,6},{3,7},{4,0},{5,1},{6,2},{7,3},{8,12},{9,13},{10,... | collective-permute-start | bytes 835592 | tf_op jit(solution)/shard_map/ppermute | solution.py:21
  299.7 22.8 %collective-permute-start.4 = (bf16[1088,256]{1,0:T(8,128)(2,1)S(1)}, bf16[1088,256]{1,0:T(8,128)(2,1)S(1)}, u32[]{:S(2)}, u32[]{:S(2)}) collective-permute-start(bf16[1088,256]{1,0:T(8,128)(2,1)S(1)} %pad_maximum_fusion.5), channel_id=1, source_target_pairs={{0,2},{1,3},{2,0},{3,1},{4,6},{5,7},{6,4},{7,5},{8,10},{9,11},{10,... | collective-permute-start | bytes 1671176 | tf_op jit(solution)/shard_map/ppermute | solution.py:21
  305.8 28.6 %collective-permute-start.11 = (bf16[1088,256]{1,0:T(8,128)(2,1)S(1)}, bf16[1088,256]{1,0:T(8,128)(2,1)S(1)}, u32[]{:S(2)}, u32[]{:S(2)}) collective-permute-start(bf16[1088,256]{1,0:T(8,128)(2,1)S(1)} %pad_maximum_fusion.6), channel_id=1, source_target_pairs={{0,2},{1,3},{2,0},{3,1},{4,6},{5,7},{6,4},{7,5},{8,10},{9,11},{10,... | collective-permute-start | bytes 1671176 | tf_op jit(solution)/shard_map/ppermute | solution.py:21
  310.6 35.6 %collective-permute-start.17 = (bf16[1088,256]{1,0:T(8,128)(2,1)S(1)}, bf16[1088,256]{1,0:T(8,128)(2,1)S(1)}, u32[]{:S(2)}, u32[]{:S(2)}) collective-permute-start(bf16[1088,256]{1,0:T(8,128)(2,1)S(1)} %pad_maximum_fusion.7), channel_id=1, source_target_pairs={{0,2},{1,3},{2,0},{3,1},{4,6},{5,7},{6,4},{7,5},{8,10},{9,11},{10,... | collective-permute-start | bytes 1671176 | tf_op jit(solution)/shard_map/ppermute | solution.py:21
  322.7 24.7 %collective-permute-start.5 = (bf16[1088,512]{1,0:T(8,128)(2,1)S(1)}, bf16[1088,512]{1,0:T(8,128)(2,1)S(1)}, u32[]{:S(2)}, u32[]{:S(2)}) collective-permute-start(bf16[1088,512]{1,0:T(8,128)(2,1)S(1)} %pad_maximum_fusion.2), channel_id=1, source_target_pairs={{0,1},{1,0},{2,3},{3,2},{4,5},{5,4},{6,7},{7,6},{8,9},{9,8},{10,11... | collective-permute-start | bytes 3342344 | tf_op jit(solution)/shard_map/ppermute | solution.py:21
  336.5 22.9 %collective-permute-start.12 = (bf16[1088,512]{1,0:T(8,128)(2,1)}, bf16[1088,512]{1,0:T(8,128)(2,1)}, u32[]{:S(2)}, u32[]{:S(2)}) collective-permute-start(bf16[1088,512]{1,0:T(8,128)(2,1)} %pad_maximum_fusion.3), channel_id=1, source_target_pairs={{0,1},{1,0},{2,3},{3,2},{4,5},{5,4},{6,7},{7,6},{8,9},{9,8},{10,11... | collective-permute-start | bytes 3342344 | tf_op jit(solution)/shard_map/ppermute | solution.py:21
  353.6 60.2 %all-to-all-start.1 = ((bf16[32,34,896]{2,1,0:T(8,128)(2,1)}), bf16[32,34,896]{2,1,0:T(8,128)(2,1)S(1)}, u32[]{:S(2)}, u32[]{:S(2)}) async-start(bf16[32,34,896]{2,1,0:T(8,128)(2,1)} %reshape.137), calls=%async_computation.1 | async-start | bytes 4587520 | tf_op jit(solution)/shard_map/all_to_all | solution.py:194
  413.8 61.1 %all-to-all-start.4 = ((bf16[32,34,896]{2,1,0:T(8,128)(2,1)}), bf16[32,34,896]{2,1,0:T(8,128)(2,1)}, u32[]{:S(2)}, u32[]{:S(2)}) async-start(bf16[32,34,896]{2,1,0:T(8,128)(2,1)} %reshape.144), calls=%async_computation.4 | async-start | bytes 4587520 | tf_op jit(solution)/shard_map/all_to_all | solution.py:228
  438.9 80.8 %collective-permute-start.6 = (bf16[64,7168]{1,0:T(8,128)(2,1)}, bf16[64,7168]{1,0:T(8,128)(2,1)}, u32[]{:S(2)}, u32[]{:S(2)}) collective-permute-start(bf16[64,7168]{1,0:T(8,128)(2,1)} %fusion.1), channel_id=1, source_target_pairs={{0,32},{32,64},{64,96},{96,128},{128,160},{160,192},{192,224},{1,3... | collective-permute-start | bytes 2752520 | tf_op jit(solution)/shard_map/ppermute | solution.py:27
  484.0 35.7 %collective-permute-start.19 = (bf16[64,7168]{1,0:T(8,128)(2,1)S(1)}, bf16[64,7168]{1,0:T(8,128)(2,1)S(1)}, u32[]{:S(2)}, u32[]{:S(2)}) collective-permute-start(bf16[64,7168]{1,0:T(8,128)(2,1)S(1)} %fusion.41), channel_id=1, source_target_pairs={{32,0},{64,32},{96,64},{128,96},{160,128},{192,160},{224,192},{33,... | collective-permute-start | bytes 2752520 | tf_op jit(solution)/shard_map/ppermute | solution.py:27
  (35 other events, 341.0 us)

commit v2 on v1

v2 whole, which is shorter than its diff:
```python
import math

import jax
import jax.numpy as jnp
from jax import lax
from jax.experimental import pallas as pl
from jax.experimental.pallas import tpu as pltpu
from jax.sharding import PartitionSpec as P

D = 7168
HID = 1024
EXPERTS = 4
PARTS = 8
PEERS = EXPERTS * PARTS
TOK = 64
MAIN = 32
TILE = 16
WIDTH = D // PARTS
BLOCKS = WIDTH // 128
ROWS_MAIN = PEERS * MAIN
ROWS_LEFT = PEERS * 2
ROWS = ROWS_MAIN + ROWS_LEFT
FOLDED = PEERS * TILE
N_PIPE = 8

qlimit = 7.0
epsilon = 1e-06
MESH = pl.DeviceIdType.MESH
F32 = jnp.float32
BF16 = jnp.bfloat16

SIN_PI = (3.1415927410125732, -5.167710304260254, 2.550077438354492, -0.598291277885437, 0.07765766233205795)
COS_PI = (
    1.0,
    -4.934802055358887,
    4.058709144592285,
    -1.335211992263794,
    0.23493731021881104,
    -0.024396324530243874,
)
NN = (((1,), (0,)), ((), ()))
NT = (((1,), (1,)), ((), ()))
TN = (((0,), (0,)), ((), ()))
U, C, A = 0, 1, 2


def dot(a, b, dims=NN):
    return lax.dot_general(a, b, dims, preferred_element_type=F32)


def poly(coefs, square):
    total = coefs[-1]
    for coef in coefs[-2::-1]:
        total = total * square + coef
    return total


def waves(weights, inverse):
    ratio = weights.astype(F32) * inverse
    clipped = jnp.clip(ratio, -qlimit, qlimit)
    rest = clipped - jnp.round(clipped)
    square = rest * rest
    sine = rest * poly(SIN_PI, square)
    return clipped, jnp.abs(ratio) < qlimit, sine, sine * poly(COS_PI, square) * (1.0 / math.pi)


def iota(shape, axis):
    return lax.broadcasted_iota(jnp.int32, shape, axis)


def at(index, size):
    return pl.ds(pl.multiple_of(index * size, size), size)


def pack_tables(routes, gates):
    members = jnp.concatenate(
        [((routes[0:1] == e) | (routes[1:2] == e)).astype(F32) for e in range(EXPERTS)]
        + [jnp.zeros((EXPERTS, TOK), F32)],
        axis=0,
    )
    earlier = (iota((TOK, TOK), 0) < iota((TOK, TOK), 1)).astype(F32)
    slots = dot(members.astype(BF16), earlier.astype(BF16))
    main, left, main_gate, left_gate = [], [], [], []
    for e in range(EXPERTS):
        gate = jnp.where(routes[0:1] == e, gates[0:1], 0.0) + jnp.where(
            routes[1:2] == e, gates[1:2], 0.0
        )
        named = members[e : e + 1] > 0.5
        slot = slots[e : e + 1].astype(jnp.int32)
        for rows, tables, gated in ((MAIN, main, main_gate), (TILE, left, left_gate)):
            place = iota((rows, TOK), 0)
            if rows == TILE:
                place = MAIN + lax.rem(place, 2)
            table = ((place == slot) & named).astype(F32)
            tables.append(table)
            gated.append(jnp.sum(table * gate, axis=1, keepdims=True))
    table = jnp.concatenate(main + left, axis=0).astype(BF16)
    return table, jnp.concatenate(main_gate + left_gate, axis=0)


def unpack_tables(routes, gates):
    lane = iota((TOK, 128), 1).astype(F32)
    members = ((lane == routes[:, 0:1]) | (lane == routes[:, 1:2])).astype(F32)
    earlier = (iota((TOK, TOK), 0) > iota((TOK, TOK), 1)).astype(F32)
    slots = dot(earlier.astype(BF16), members.astype(BF16)).astype(jnp.int32)
    main = jnp.zeros((TOK, EXPERTS * MAIN), F32)
    folded = jnp.zeros((TOK, EXPERTS * TILE), F32)
    lane_main = iota(main.shape, 1)
    lane_fold = iota(folded.shape, 1)
    for e in range(EXPERTS):
        if gates is None:
            value = members[:, e : e + 1]
        else:
            value = jnp.where(routes[:, 0:1] == e, gates[:, 0:1], 0.0) + jnp.where(
                routes[:, 1:2] == e, gates[:, 1:2], 0.0
            )
        slot = slots[:, e : e + 1]
        main = main + jnp.where(lane_main == e * MAIN + slot, jnp.where(slot < MAIN, value, 0.0), 0.0)
        here = (lax.div(lane_fold, TILE) == e) & (MAIN + lax.rem(lane_fold, 2) == slot)
        folded = folded + jnp.where(here, value, 0.0)
    block = lax.div(lax.rem(lane_fold, TILE), 2)
    folded = jnp.concatenate([jnp.where(block == b, folded, 0.0) for b in range(BLOCKS)], axis=0)
    return main, folded


def terms(table, count):
    out = []
    for _ in range(count):
        out.append(table.astype(BF16))
        table = table - out[-1].astype(F32)
    return out


def kernel(
    xa, xb, cb, by_row, by_col, w_up, w_down, s_up, s_down,
    o_next, o_cot, o_up, o_down, o_sums,
    q_up, q_down, rows, folds, snd, snd_fold, ret, ret_fold,
    keep, send1, recv1, send2, recv2, send3, recv3, gathered,
    out_a, out_b, g_wide, unit_a, unit_b, sum_snd, sum_rcv,
    d_ss, d_rs, d_sf, d_rf, h_s, h_r, g_s, g_r, t_ss, t_rs, t_sf, t_rf, p_s, p_r, z_s, z_r,
):
    me = lax.axis_index("expert")
    pipe = lax.axis_index("pipe")
    mine = me // PARTS
    part = me % PARTS
    bits = (part % 2, (part // 2) % 2, part // 4)
    partners = [me + (1 << k) - (2 << k) * bits[k] for k in range(3)]

    barrier = pltpu.get_barrier_semaphore()

    @pl.loop(1, PEERS)
    def _(i):
        pl.semaphore_signal(barrier, inc=1, device_id=(pipe, (me + i) % PEERS), device_id_type=MESH)

    @pl.when(pipe > 0)
    def _():
        pl.semaphore_signal(barrier, inc=1, device_id=(pipe - 1, me), device_id_type=MESH)

    @pl.when(pipe < N_PIPE - 1)
    def _():
        pl.semaphore_signal(barrier, inc=1, device_id=(pipe + 1, me), device_id_type=MESH)

    def copy(src, dst, send_sem, recv_sem, to, along=None):
        return pltpu.make_async_remote_copy(
            src_ref=src,
            dst_ref=dst,
            send_sem=send_sem,
            recv_sem=recv_sem,
            device_id=(pipe if along is None else along, to),
            device_id_type=MESH,
        )

    def wait_for(ref, sem):
        pltpu.make_async_copy(ref, ref, sem).wait()

    def norm_of(x_ref, unit):
        def body(q, total):
            wide = x_ref[:, at(q, WIDTH)].astype(F32)
            return total + jnp.sum(wide * wide, axis=1, keepdims=True)

        total = lax.fori_loop(0, PARTS, body, jnp.zeros((TOK, 1), F32))
        unit[...] = jnp.broadcast_to(lax.rsqrt(total * (1.0 / D) + epsilon), unit.shape)

    fold_row = lax.div(lax.rem(iota((EXPERTS * TILE, 128), 0), TILE), 2)

    def dispatch(kind, slot, x_ref, table, unit, gate):
        def pack(q):
            values = x_ref[:, at(q, WIDTH)]
            if unit is not None:
                values = (values.astype(F32) * unit[:, 0:1]).astype(BF16)
            packed = dot(table, values)
            if gate is not None:
                packed = packed * gate
            left = jnp.zeros((EXPERTS * TILE, 128), F32)
            for b in range(BLOCKS):
                part_b = packed[EXPERTS * MAIN :, b * 128 : (b + 1) * 128]
                left = jnp.where(fold_row == b, part_b, left)
            for e in range(EXPERTS):
                to = e * PARTS + q
                snd[slot, at(to, MAIN), :] = packed[e * MAIN : (e + 1) * MAIN].astype(BF16)
                snd_fold[slot, at(to, TILE), :] = left[e * TILE : (e + 1) * TILE].astype(BF16)

        def send(to):
            copy(
                snd.at[slot, at(to, MAIN)], rows.at[kind, at(me, MAIN)], d_ss.at[slot], d_rs.at[kind], to
            ).start()
            copy(
                snd_fold.at[slot, at(to, TILE)], folds.at[kind, at(me, TILE)], d_sf.at[slot], d_rf.at[kind], to
            ).start()

        @pl.loop(1, PARTS)
        def _(s):
            q = (part + s) % PARTS
            pack(q)
            for r in range(EXPERTS):
                send(((mine + r) % EXPERTS) * PARTS + q)

        pack(part)
        for r in range(1, EXPERTS):
            send(((mine + r) % EXPERTS) * PARTS + part)
        rows[kind, at(me, MAIN), :] = snd[slot, at(me, MAIN), :]
        folds[kind, at(me, TILE), :] = snd_fold[slot, at(me, TILE), :]

    others_main = pl.ds(0, (PEERS - 1) * MAIN)
    others_fold = pl.ds(0, (PEERS - 1) * TILE)

    def sent(slot):
        wait_for(snd.at[slot, others_main], d_ss.at[slot])
        wait_for(snd_fold.at[slot, others_fold], d_sf.at[slot])

    def arrive(kind):
        wait_for(rows.at[kind, others_main], d_rs.at[kind])
        wait_for(folds.at[kind, others_fold], d_rf.at[kind])
        shape = (BLOCKS * ROWS_LEFT, FOLDED)
        to, come = iota(shape, 0), iota(shape, 1)
        place = lax.rem(to, ROWS_LEFT)
        wanted = lax.div(place, 2) * TILE + lax.div(to, ROWS_LEFT) * 2 + lax.rem(place, 2)
        spread = dot((come == wanted).astype(BF16), folds[kind])
        for b in range(BLOCKS):
            rows[kind, pl.ds(ROWS_MAIN, ROWS_LEFT), b * 128 : (b + 1) * 128] = spread[
                b * ROWS_LEFT : (b + 1) * ROWS_LEFT
            ].astype(BF16)

    def row_chunks(body):
        @pl.loop(0, 4)
        def _(i):
            body(at(i, 256), i)

        body(pl.ds(ROWS_MAIN, ROWS_LEFT), None)

    def step_1(kind, held):
        def body(chunk, _):
            lhs = rows[kind, chunk, :]
            for k in range(4):
                span = slice(k * 256, (k + 1) * 256)
                both = dot(lhs, q_down[span, :], NT) if kind == C else dot(lhs, q_up[:, span])
                low, high = both[:, :128], both[:, 128:]
                odd = bits[0] == 1
                keep[held, k, chunk, :] = jnp.where(odd, high, low)
                send1[kind, k, chunk, :] = jnp.where(odd, low, high).astype(BF16)

        row_chunks(body)
        copy(send1.at[kind], recv1.at[kind], h_s.at[0, kind], h_r.at[0, kind], partners[0]).start()

    def step_2(kind, held):
        wait_for(recv1.at[kind], h_r.at[0, kind])
        for m in range(2):
            give = 2 * m + 1 - bits[1]
            send2[kind, m] = (keep[held, give] + recv1[kind, give].astype(F32)).astype(BF16)
        copy(send2.at[kind], recv2.at[kind], h_s.at[1, kind], h_r.at[1, kind], partners[1]).start()
        for m in range(2):
            own = 2 * m + bits[1]
            keep[held, own] = keep[held, own] + recv1[kind, own].astype(F32)

    def step_3(kind, held):
        wait_for(recv2.at[kind], h_r.at[1, kind])
        give = 1 - bits[2]
        send3[kind] = (keep[held, 2 * give + bits[1]] + recv2[kind, give].astype(F32)).astype(BF16)
        copy(send3.at[kind], recv3.at[kind], h_s.at[2, kind], h_r.at[2, kind], partners[2]).start()

    def summed(kind, held, chunk):
        own = bits[2]
        total = keep[held, 2 * own + bits[1], chunk, :] + recv2[kind, own, chunk, :].astype(F32)
        return (total + recv3[kind, chunk, :].astype(F32)).astype(BF16).astype(F32)

    def gather(kind, step):
        if step == 0:
            blocks = [part]
        elif step == 1:
            blocks = [bits[0] + 2 * bits[1], bits[0] + 2 * bits[1] + 4]
        else:
            blocks = [2 * k + bits[0] for k in range(4)]
        for block in blocks:
            copy(
                gathered.at[kind, block], gathered.at[kind, block],
                g_s.at[step, kind], g_r.at[step, kind], partners[2 - step],
            ).start()

    def gather_wait(kind, step):
        wait_for(gathered.at[kind, pl.ds(0, 1 << step)], g_r.at[step, kind])

    def wide(kind, chunk):
        return jnp.concatenate([gathered[kind, j, chunk, :] for j in range(PARTS)], axis=1)

    def give_back(slot, made):
        @pl.loop(0, 4)
        def _(i):
            snd[slot, at(i, 256), :] = made(at(i, 256)).astype(BF16)

        left = made(pl.ds(ROWS_MAIN, ROWS_LEFT)).astype(BF16)
        shape = (FOLDED, BLOCKS * ROWS_LEFT)
        to, come = iota(shape, 0), iota(shape, 1)
        inner = lax.rem(to, TILE)
        wanted = lax.div(inner, 2) * ROWS_LEFT + lax.div(to, TILE) * 2 + lax.rem(inner, 2)
        stacked = jnp.concatenate([left[:, b * 128 : (b + 1) * 128] for b in range(BLOCKS)], axis=0)
        snd_fold[slot] = dot((come == wanted).astype(BF16), stacked).astype(BF16)

        def send(to):
            copy(
                snd.at[slot, at(to, MAIN)], ret.at[slot, at(me, MAIN)], t_ss.at[slot], t_rs.at[slot, part], to
            ).start()
            copy(
                snd_fold.at[slot, at(to, TILE)], ret_fold.at[slot, at(me, TILE)],
                t_sf.at[slot], t_rf.at[slot, part], to,
            ).start()

        @pl.loop(1, PEERS)
        def _(i):
            send((me + i) % PEERS)

        ret[slot, at(me, MAIN), :] = snd[slot, at(me, MAIN), :]
        ret_fold[slot, at(me, TILE), :] = snd_fold[slot, at(me, TILE), :]

    def come_back(slot, q, count):
        wait_for(ret.at[slot, pl.ds(0, count * MAIN)], t_rs.at[slot, q])
        wait_for(ret_fold.at[slot, pl.ds(0, count * TILE)], t_rf.at[slot, q])

    def combined(slot, q, mains, foldeds):
        come = jnp.concatenate([ret[slot, at(e * PARTS + q, MAIN), :] for e in range(EXPERTS)], axis=0)
        fold = jnp.concatenate([ret_fold[slot, at(e * PARTS + q, TILE), :] for e in range(EXPERTS)], axis=0)
        total = sum(dot(table, come) for table in mains)
        extra = sum(dot(table, fold) for table in foldeds)
        return total + jnp.concatenate([extra[b * TOK : (b + 1) * TOK] for b in range(BLOCKS)], axis=1)

    table_b, gate_b = pack_tables(by_row[4:6, :], by_row[6:8, :])
    norm_of(xb, unit_b)
    pl.semaphore_wait(
        barrier, PEERS - 1 + jnp.where(pipe > 0, 1, 0) + jnp.where(pipe < N_PIPE - 1, 1, 0)
    )
    dispatch(U, 0, xb, table_b, unit_b, None)
    dispatch(C, 1, cb, table_b, None, gate_b)

    step_up, step_down = s_up[0, mine], s_down[0, mine]
    one = jnp.ones((1, 1), F32)
    inv_up, inv_down = one / step_up, one / step_down

    @pl.loop(0, WIDTH // 64)
    def _(i):
        ratio, _, _, bend = waves(w_up[at(i, 64), :], inv_up)
        q_up[at(i, 64), :] = (step_up * (ratio - bend)).astype(BF16)

    @pl.loop(0, HID // 64)
    def _(i):
        ratio, _, _, bend = waves(w_down[at(i, 64), :], inv_down)
        q_down[at(i, 64), :] = (step_down * (ratio - bend)).astype(BF16)

    table_a, _ = pack_tables(by_row[0:2, :], by_row[2:4, :])
    norm_of(xa, unit_a)

    arrive(U)
    step_1(U, 0)
    sent(0)
    dispatch(A, 0, xa, table_a, unit_a, None)
    arrive(C)
    step_1(C, 1)
    step_2(U, 0)
    step_2(C, 1)
    step_3(U, 0)
    step_3(C, 1)
    wait_for(recv3.at[U], h_r.at[2, U])
    wait_for(recv3.at[C], h_r.at[2, C])

    def between(chunk, _):
        pre = summed(U, 0, chunk)
        grad = summed(C, 1, chunk)
        sigma = 1.0 / (1.0 + jnp.exp(-pre))
        gathered[U, part, chunk, :] = (grad * (sigma * (1.0 + pre * (1.0 - sigma)))).astype(BF16)
        gathered[C, part, chunk, :] = (pre * sigma).astype(BF16)

    row_chunks(between)
    gather(U, 0)
    gather(C, 0)
    arrive(A)
    step_1(A, 0)
    gather_wait(U, 0)
    gather(U, 1)
    gather_wait(C, 0)
    gather(C, 1)
    step_2(A, 0)
    gather_wait(U, 1)
    gather(U, 2)
    gather_wait(C, 1)
    gather(C, 2)
    step_3(A, 0)
    gather_wait(U, 2)
    sent(1)
    give_back(1, lambda chunk: dot(wide(U, chunk), q_up[...], NT))

    wait_for(recv3.at[A], h_r.at[2, A])

    def silu_rows(chunk, _):
        pre = summed(A, 0, chunk)
        gathered[A, part, chunk, :] = (pre / (1.0 + jnp.exp(-pre))).astype(BF16)

    row_chunks(silu_rows)
    gather(A, 0)
    gather_wait(A, 0)
    gather(A, 1)
    gather_wait(A, 1)
    gather(A, 2)
    gather_wait(C, 2)
    gather_wait(A, 2)
    sent(0)
    give_back(0, lambda chunk: dot(wide(A, chunk), q_down[...]))

    def quant_grads(weights, inverse, grads):
        ratio, inside, sine, bend = waves(weights, inverse)
        wave = jnp.where(inside, 2.0 * sine * sine, 0.0)
        grads = grads.astype(BF16).astype(F32)
        return (grads * wave).astype(BF16), jnp.sum(
            grads * (ratio - bend - ratio * wave), axis=0, keepdims=True
        )

    def up_body(i, total):
        lhs = rows[U, :, at(i, 128)]
        for k in range(4):
            rhs = jnp.concatenate([gathered[U, 2 * k], gathered[U, 2 * k + 1]], axis=1)
            span = slice(k * 256, (k + 1) * 256)
            out, partial = quant_grads(w_up[at(i, 128), span], inv_up, dot(lhs, rhs, TN))
            o_up[at(i, 128), span] = out
            total = total + partial
        return total

    def down_body(j, total):
        out, partial = quant_grads(w_down[at(j, 128), :], inv_down, dot(gathered[C, j], rows[C], TN))
        o_down[at(j, 128), :] = out
        return total + partial

    up_total = lax.fori_loop(0, BLOCKS, up_body, jnp.zeros((1, 256), F32))
    down_total = lax.fori_loop(0, PARTS, down_body, jnp.zeros((1, WIDTH), F32))
    first = iota((8, 128), 0) == 0
    scaled = 1.0 / math.sqrt(D * HID * qlimit)
    sum_snd[...] = (
        jnp.where(
            first,
            jnp.sum(up_total, axis=1, keepdims=True),
            jnp.sum(down_total, axis=1, keepdims=True),
        )
        * scaled
    )
    sum_rcv[me] = sum_snd[...]

    @pl.loop(1, PEERS)
    def _(i):
        copy(sum_snd, sum_rcv.at[me], z_s, z_r, (me + i) % PEERS).start()

    main_b, fold_b = unpack_tables(by_col[:, 4:6], None)
    main_b, fold_b = terms(main_b, 1), terms(fold_b, 1)

    def take_b(q):
        grads = combined(1, q, main_b, fold_b)
        g_wide[:, at(q, WIDTH)] = grads
        return jnp.sum(xb[:, at(q, WIDTH)].astype(F32) * grads, axis=1, keepdims=True)

    come_back(1, part, EXPERTS - 1)
    along = take_b(part)

    def body_b(s, total):
        q = (part + s) % PARTS
        come_back(1, q, EXPERTS)
        return total + take_b(q)

    along = lax.fori_loop(1, PARTS, body_b, along)
    unit = unit_b[:, 0:1]
    bent = along * unit * unit * unit * (1.0 / D)

    @pl.loop(0, PARTS)
    def _(q):
        span = at(q, WIDTH)
        back = g_wide[:, span] * unit - xb[:, span].astype(F32) * bent
        out_b[:, span] = (cb[:, span].astype(F32) + back).astype(BF16)

        @pl.when(pipe > 0)
        def _():
            copy(out_b.at[:, span], o_cot.at[:, span], p_s.at[1], p_r.at[1], me, pipe - 1).start()

    main_a, fold_a = unpack_tables(by_col[:, 0:2], by_col[:, 2:4])
    main_a, fold_a = terms(main_a, 3), terms(fold_a, 3)

    def take_a(q):
        span = at(q, WIDTH)
        out_a[:, span] = (xa[:, span].astype(F32) + combined(0, q, main_a, fold_a)).astype(BF16)

        @pl.when(pipe < N_PIPE - 1)
        def _():
            copy(out_a.at[:, span], o_next.at[:, span], p_s.at[0], p_r.at[0], me, pipe + 1).start()

    come_back(0, part, EXPERTS - 1)
    take_a(part)

    @pl.loop(1, PARTS)
    def _(s):
        q = (part + s) % PARTS
        come_back(0, q, EXPERTS)
        take_a(q)

    wait_for(sum_rcv.at[pl.ds(0, PEERS - 1)], z_r)
    for e in range(EXPERTS):
        o_sums[e] = sum(sum_rcv[e * PARTS + k] for k in range(PARTS))

    wait_for(sum_rcv.at[pl.ds(0, PEERS - 1)], z_s)
    for slot in (0, 1):
        wait_for(snd.at[slot, others_main], t_ss.at[slot])
        wait_for(snd_fold.at[slot, others_fold], t_sf.at[slot])
    for kind in (U, C, A):
        wait_for(send1.at[kind], h_s.at[0, kind])
        wait_for(send2.at[kind], h_s.at[1, kind])
        wait_for(send3.at[kind], h_s.at[2, kind])
        for step in range(3):
            wait_for(gathered.at[kind, pl.ds(0, 1 << step)], g_s.at[step, kind])

    @pl.when(pipe > 0)
    def _():
        wait_for(out_b, p_s.at[1])
        wait_for(o_next, p_r.at[0])

    @pl.when(pipe == 0)
    def _():
        o_next[...] = jnp.zeros_like(o_next)

    @pl.when(pipe < N_PIPE - 1)
    def _():
        wait_for(out_a, p_s.at[0])
        wait_for(o_cot, p_r.at[1])

    @pl.when(pipe == N_PIPE - 1)
    def _():
        o_cot[...] = jnp.zeros_like(o_cot)


def shards(
    acts_a, acts_b, cot_b, routes_a, gates_a, routes_b, gates_b, up_weight, down_weight, up_scale, down_scale
):
    by_col = jnp.concatenate(
        (routes_a[0].astype(F32), gates_a[0], routes_b[0].astype(F32), gates_b[0]), axis=1
    )
    vmem = pl.BlockSpec(memory_space=pltpu.VMEM)
    smem = pl.BlockSpec(memory_space=pltpu.SMEM)
    dma = pltpu.SemaphoreType.DMA

    def bf(*shape):
        return pltpu.VMEM(shape, BF16)

    def wide(*shape):
        return pltpu.VMEM(shape, F32)

    def out(*shape):
        return jax.ShapeDtypeStruct(shape, BF16)

    next_a, next_cot, dw_up, dw_down, sums = pl.pallas_call(
        kernel,
        out_shape=(
            out(TOK, D), out(TOK, D), out(WIDTH, HID), out(HID, WIDTH),
            jax.ShapeDtypeStruct((EXPERTS, 8, 128), F32),
        ),
        in_specs=[vmem] * 7 + [smem] * 2,
        out_specs=(vmem,) * 5,
        scratch_shapes=[
            bf(WIDTH, HID), bf(HID, WIDTH),
            bf(3, ROWS, WIDTH), bf(3, FOLDED, 128),
            bf(2, ROWS_MAIN, WIDTH), bf(2, FOLDED, 128),
            bf(2, ROWS_MAIN, WIDTH), bf(2, FOLDED, 128),
            wide(2, 4, ROWS, 128),
            bf(3, 4, ROWS, 128), bf(3, 4, ROWS, 128),
            bf(3, 2, ROWS, 128), bf(3, 2, ROWS, 128),
            bf(3, ROWS, 128), bf(3, ROWS, 128),
            bf(3, PARTS, ROWS, 128),
            bf(TOK, D), bf(TOK, D), wide(TOK, D),
            wide(TOK, 128), wide(TOK, 128),
            wide(8, 128), wide(PEERS, 8, 128),
            dma((2,)), dma((3,)), dma((2,)), dma((3,)),
            dma((3, 3)), dma((3, 3)), dma((3, 3)), dma((3, 3)),
            dma((2,)), dma((2, PARTS)), dma((2,)), dma((2, PARTS)),
            dma((2,)), dma((2,)), dma, dma,
        ],
        compiler_params=pltpu.CompilerParams(
            collective_id=0, has_side_effects=True, vmem_limit_bytes=62 << 20
        ),
    )(
        acts_a[0], acts_b[0], cot_b[0], by_col.T, by_col, up_weight[0], down_weight[0], up_scale, down_scale
    )
    return (
        next_a[None], next_cot[None], dw_up[None], dw_down[None], sums[None, :, 0, 0], sums[None, :, 1, 0],
    )


def solution(mesh):
    split, rows = P("pipe", "expert", None), P("pipe", None)
    columns = P("pipe", None, "expert")
    return jax.shard_map(
        shards,
        mesh=mesh,
        in_specs=(split,) * 8 + (columns, rows, rows),
        out_specs=(split, split, split, columns, rows, rows),
        check_vma=False,
    )
```

time: 531 us -> 414 us (0.78)
  the two profiles are of different devices: /device:TPU:16 before, /device:TPU:217 now
where the time goes in v2:
time: 414 us
  Pallas kernels  403 us (97%)
  local copies, waits for them, and re-layouts  8.75 us (2%)
    pallas_call x1, Pallas kernels, shards(): pl.pallas_call(kernel, out_shape=(out(TOK, D), out(TOK, D), out(WIDTH, HI...  403 us

profile of v2, /device:TPU:217, one launch (start us, length us, event | category | flops | bytes accessed | tf_op | source)
XLA Modules:
  0.0 414.2 jit_solution(5305245147515945708)
XLA Ops:
  0.6 0.7 convert_bitcast_fusion
  1.3 1.3 pad_maximum_fusion
  2.6 0.7 copy.27.by_col
  3.3 402.8 %shard_map.154 = (bf16[64,7168]{1,0:T(8,128)(2,1)}, bf16[64,7168]{1,0:T(8,128)(2,1)}, bf16[896,1024]{1,0:T(8,128)(2,1)}, bf16[1024,896]{1,0:T(8,128)(2,1)}, f32[4,8,128]{2,1,0:T(8,128)}) custom-call(bf16[64,7168]{1,0:T(8,128)(2,1)} %bitcast.23, bf16[64,7168]{1,0:T(8,128)(2,1)} %bitcast.24, bf16[64,7168]{1,0:T(8,128)(2,1)} %bitcast.25, ...), custom_call_target="tpu_custom_call" | custom-call | tf_op jit(solution)/shard_map/pallas_call | solution.py:570
  406.1 0.0 copy-start.2
  406.1 1.4 slice_reduce_fusion
  407.5 0.0 copy-start.1
  407.5 2.3 copy.32
  409.8 0.0 copy-done.2
  409.8 0.9 copy.33
  410.8 0.0 copy-done.1
  410.8 0.0 copy-start
  410.8 1.2 copy.34
  412.0 0.9 copy-done
  412.9 1.2 copy.35
Async XLA Ops:
  406.1 3.8 copy-start.2
  407.5 3.2 copy-start.1
  410.8 2.2 copy-start

commit v3 on v2

--- a/solution.py
+++ b/solution.py
@@ -22,6 +22,7 @@
 ROWS = ROWS_MAIN + ROWS_LEFT
 FOLDED = PEERS * TILE
 N_PIPE = 8
+PIECES = 4
 
 qlimit = 7.0
 epsilon = 1e-06
@@ -135,16 +136,19 @@
     xa, xb, cb, by_row, by_col, w_up, w_down, s_up, s_down,
     o_next, o_cot, o_up, o_down, o_sums,
     q_up, q_down, rows, folds, snd, snd_fold, ret, ret_fold,
-    keep, send1, recv1, send2, recv2, send3, recv3, gathered,
+    keep, send1, recv1, passed, gathered,
     out_a, out_b, g_wide, unit_a, unit_b, sum_snd, sum_rcv,
-    d_ss, d_rs, d_sf, d_rf, h_s, h_r, g_s, g_r, t_ss, t_rs, t_sf, t_rf, p_s, p_r, z_s, z_r,
+    d_ss, d_rs, d_sf, d_rf, h_s, h_r, l_s, l_r, g_s, g_r, c_s, c_r, t_ss, t_rs, t_sf, t_rf, p_s, p_r, z_s, z_r,
 ):
     me = lax.axis_index("expert")
     pipe = lax.axis_index("pipe")
     mine = me // PARTS
     part = me % PARTS
-    bits = (part % 2, (part // 2) % 2, part // 4)
-    partners = [me + (1 << k) - (2 << k) * bits[k] for k in range(3)]
+    core, chip = part % 2, part // 2
+    other_core = me + 1 - 2 * core
+    upper = chip // 2
+    is_end = (chip % 3) == 0
+    over, away = me + 2 - 4 * upper, me - 2 + 4 * upper
 
     barrier = pltpu.get_barrier_semaphore()
 
@@ -255,49 +259,87 @@
                 span = slice(k * 256, (k + 1) * 256)
                 both = dot(lhs, q_down[span, :], NT) if kind == C else dot(lhs, q_up[:, span])
                 low, high = both[:, :128], both[:, 128:]
-                odd = bits[0] == 1
+                odd = core == 1
                 keep[held, k, chunk, :] = jnp.where(odd, high, low)
                 send1[kind, k, chunk, :] = jnp.where(odd, low, high).astype(BF16)
 
         row_chunks(body)
-        copy(send1.at[kind], recv1.at[kind], h_s.at[0, kind], h_r.at[0, kind], partners[0]).start()
-
-    def step_2(kind, held):
-        wait_for(recv1.at[kind], h_r.at[0, kind])
-        for m in range(2):
-            give = 2 * m + 1 - bits[1]
-            send2[kind, m] = (keep[held, give] + recv1[kind, give].astype(F32)).astype(BF16)
-        copy(send2.at[kind], recv2.at[kind], h_s.at[1, kind], h_r.at[1, kind], partners[1]).start()
-        for m in range(2):
-            own = 2 * m + bits[1]
-            keep[held, own] = keep[held, own] + recv1[kind, own].astype(F32)
-
-    def step_3(kind, held):
-        wait_for(recv2.at[kind], h_r.at[1, kind])
-        give = 1 - bits[2]
-        send3[kind] = (keep[held, 2 * give + bits[1]] + recv2[kind, give].astype(F32)).astype(BF16)
-        copy(send3.at[kind], recv3.at[kind], h_s.at[2, kind], h_r.at[2, kind], partners[2]).start()
-
-    def summed(kind, held, chunk):
-        own = bits[2]
-        total = keep[held, 2 * own + bits[1], chunk, :] + recv2[kind, own, chunk, :].astype(F32)
-        return (total + recv3[kind, chunk, :].astype(F32)).astype(BF16).astype(F32)
-
-    def gather(kind, step):
-        if step == 0:
-            blocks = [part]
-        elif step == 1:
-            blocks = [bits[0] + 2 * bits[1], bits[0] + 2 * bits[1] + 4]
-        else:
-            blocks = [2 * k + bits[0] for k in range(4)]
-        for block in blocks:
-            copy(
-                gathered.at[kind, block], gathered.at[kind, block],
-                g_s.at[step, kind], g_r.at[step, kind], partners[2 - step],
-            ).start()
-
-    def gather_wait(kind, step):
-        wait_for(gathered.at[kind, pl.ds(0, 1 << step)], g_r.at[step, kind])
+        copy(send1.at[kind], recv1.at[kind], h_s.at[kind], h_r.at[kind], other_core).start()
+
+    def add_core(kind, held):
+        wait_for(recv1.at[kind], h_r.at[kind])
+        wait_for(send1.at[kind], h_s.at[kind])
+
+        @pl.loop(0, 4)
+        def _(k):
+            keep[held, k] = keep[held, k] + recv1[kind, k].astype(F32)
+
+    def half(kind, held, k, rows_at, to, step, come):
+        total = keep[held, k, rows_at, :]
+        if come:
+            wait_for(passed.at[kind, k, rows_at], l_r.at[kind, k, step])
+            total = total + passed[kind, k, rows_at, :].astype(F32)
+        send1[kind, k, rows_at, :] = total.astype(BF16)
+        copy(
+            send1.at[kind, k, rows_at], passed.at[kind, k, rows_at], l_s.at[kind], l_r.at[kind, k, step], to
+        ).start()
+
+    def piece(n):
+        return pl.ds(n % 2 * (ROWS // 2), ROWS // 2)
+
+    def line_ends(kind, held):
+        @pl.when(is_end)
+        def _():
+            for n in range(PIECES):
+                half(kind, held, 2 - 2 * upper + n // 2, piece(n), over, n % 2, False)
+
+    def line_mids(kind, held, n):
+        @pl.when(jnp.logical_not(is_end))
+        def _():
+            if n < PIECES:
+                half(kind, held, 2 - 2 * upper + n // 2, piece(n), over, n % 2, True)
+            if n > 0:
+                half(kind, held, 2 * upper + (n - 1) // 2, piece(n - 1), away, (n - 1) % 2, True)
+
+    def line_come(kind, k, n):
+        wait_for(passed.at[kind, k, piece(n)], l_r.at[kind, k, n % 2])
+
+    def summed(kind, held, k, chunk):
+        total = keep[held, k, chunk, :] + passed[kind, k, chunk, :].astype(F32)
+        return total.astype(BF16).astype(F32)
+
+    def hand(kind, k, n, to):
+        span = gathered.at[kind, 2 * k + core, piece(n)]
+        copy(span, span, g_s.at[kind], g_r.at[kind, k, n % 2], to).start()
+
+    def hand_core(kind, k, n):
+        span = gathered.at[kind, 2 * k + core, piece(n)]
+        copy(span, span, c_s.at[kind], c_r.at[kind], other_core).start()
+
+    def gather_own(kind, n):
+        k = 2 * upper + n // 2
+        hand(kind, k, n, over)
+        hand_core(kind, k, n)
+
+    def gather_mids(kind, n):
+        @pl.when(jnp.logical_not(is_end))
+        def _():
+            for p, to in ((n, over), (n - 1, away)):
+                if 0 <= p < PIECES:
+                    k = (2 * upper if p == n else 2 - 2 * upper) + p // 2
+                    wait_for(gathered.at[kind, 0, piece(p)], g_r.at[kind, k, p % 2])
+                    hand(kind, k, p, to)
+                    hand_core(kind, k, p)
+
+    def gather_ends(kind):
+        @pl.when(is_end)
+        def _():
+            for n in range(PIECES):
+                k = 2 - 2 * upper + n // 2
+                wait_for(gathered.at[kind, 0, piece(n)], g_r.at[kind, k, n % 2])
+                hand_core(kind, k, n)
+
+        wait_for(gathered.at[kind, pl.ds(0, 4)], c_r.at[kind])
 
     def wide(kind, chunk):
         return jnp.concatenate([gathered[kind, j, chunk, :] for j in range(PARTS)], axis=1)
@@ -324,10 +366,13 @@
                 t_sf.at[slot], t_rf.at[slot, part], to,
             ).start()
 
-        @pl.loop(1, PEERS)
-        def _(i):
-            send((me + i) % PEERS)
-
+        @pl.loop(1, PARTS)
+        def _(s):
+            for r in range(EXPERTS):
+                send(((mine + r) % EXPERTS) * PARTS + (part + s) % PARTS)
+
+        for r in range(1, EXPERTS):
+            send(((mine + r) % EXPERTS) * PARTS + part)
         ret[slot, at(me, MAIN), :] = snd[slot, at(me, MAIN), :]
         ret_fold[slot, at(me, TILE), :] = snd_fold[slot, at(me, TILE), :]
 
@@ -373,55 +418,90 @@
     dispatch(A, 0, xa, table_a, unit_a, None)
     arrive(C)
     step_1(C, 1)
-    step_2(U, 0)
-    step_2(C, 1)
-    step_3(U, 0)
-    step_3(C, 1)
-    wait_for(recv3.at[U], h_r.at[2, U])
-    wait_for(recv3.at[C], h_r.at[2, C])
-
-    def between(chunk, _):
-        pre = summed(U, 0, chunk)
-        grad = summed(C, 1, chunk)
-        sigma = 1.0 / (1.0 + jnp.exp(-pre))
-        gathered[U, part, chunk, :] = (grad * (sigma * (1.0 + pre * (1.0 - sigma)))).astype(BF16)
-        gathered[C, part, chunk, :] = (pre * sigma).astype(BF16)
-
-    row_chunks(between)
-    gather(U, 0)
-    gather(C, 0)
+    add_core(U, 0)
+    line_ends(U, 0)
+    add_core(C, 1)
+    line_ends(C, 1)
+    for n in range(PIECES + 1):
+        line_mids(U, 0, n)
+        line_mids(C, 1, n)
+
+    @pl.when(is_end)
+    def _():
+        for n in range(PIECES):
+            k = 2 * upper + n // 2
+            chunk = piece(n)
+            line_come(U, k, n)
+            line_come(C, k, n)
+            pre = summed(U, 0, k, chunk)
+            grad = summed(C, 1, k, chunk)
+            sigma = 1.0 / (1.0 + jnp.exp(-pre))
+            gathered[U, 2 * k + core, chunk, :] = (grad * (sigma * (1.0 + pre * (1.0 - sigma)))).astype(BF16)
+            gathered[C, 2 * k + core, chunk, :] = (pre * sigma).astype(BF16)
+            gather_own(U, n)
+            gather_own(C, n)
+
     arrive(A)
     step_1(A, 0)
-    gather_wait(U, 0)
-    gather(U, 1)
-    gather_wait(C, 0)
-    gather(C, 1)
-    step_2(A, 0)
-    gather_wait(U, 1)
-    gather(U, 2)
-    gather_wait(C, 1)
-    gather(C, 2)
-    step_3(A, 0)
-    gather_wait(U, 2)
+    for n in range(2):
+        gather_mids(U, n)
+        gather_mids(C, n)
+    add_core(A, 0)
+    line_ends(A, 0)
+    for n in range(2, PIECES + 1):
+        gather_mids(U, n)
+        gather_mids(C, n)
+    for n in range(PIECES + 1):
+        line_mids(A, 0, n)
+    gather_ends(U)
     sent(1)
     give_back(1, lambda chunk: dot(wide(U, chunk), q_up[...], NT))
 
-    wait_for(recv3.at[A], h_r.at[2, A])
-
-    def silu_rows(chunk, _):
-        pre = summed(A, 0, chunk)
-        gathered[A, part, chunk, :] = (pre / (1.0 + jnp.exp(-pre))).astype(BF16)
-
-    row_chunks(silu_rows)
-    gather(A, 0)
-    gather_wait(A, 0)
-    gather(A, 1)
-    gather_wait(A, 1)
-    gather(A, 2)
-    gather_wait(C, 2)
-    gather_wait(A, 2)
+    @pl.when(is_end)
+    def _():
+        for n in range(PIECES):
+            k = 2 * upper + n // 2
+            chunk = piece(n)
+            line_come(A, k, n)
+            pre = summed(A, 0, k, chunk)
+            gathered[A, 2 * k + core, chunk, :] = (pre / (1.0 + jnp.exp(-pre))).astype(BF16)
+            gather_own(A, n)
+
+    for n in range(PIECES + 1):
+        gather_mids(A, n)
+    gather_ends(C)
+    gather_ends(A)
     sent(0)
     give_back(0, lambda chunk: dot(wide(A, chunk), q_down[...]))
+
+    main_b, fold_b = unpack_tables(by_col[:, 4:6], None)
+    main_b, fold_b = terms(main_b, 1), terms(fold_b, 1)
+
+    def take_b(q):
+        grads = combined(1, q, main_b, fold_b)
+        g_wide[:, at(q, WIDTH)] = grads
+        return jnp.sum(xb[:, at(q, WIDTH)].astype(F32) * grads, axis=1, keepdims=True)
+
+    def body_b(s, total):
+        q = (part + PARTS - s) % PARTS
+        come_back(1, q, EXPERTS)
+        return total + take_b(q)
+
+    along = lax.fori_loop(1, PARTS, body_b, jnp.zeros((TOK, 1), F32))
+    come_back(1, part, EXPERTS - 1)
+    along = along + take_b(part)
+    unit = unit_b[:, 0:1]
+    bent = along * unit * unit * unit * (1.0 / D)
+
+    @pl.loop(0, PARTS)
+    def _(q):
+        span = at(q, WIDTH)
+        back = g_wide[:, span] * unit - xb[:, span].astype(F32) * bent
+        out_b[:, span] = (cb[:, span].astype(F32) + back).astype(BF16)
+
+        @pl.when(pipe > 0)
+        def _():
+            copy(out_b.at[:, span], o_cot.at[:, span], p_s.at[1], p_r.at[1], me, pipe - 1).start()
 
     def quant_grads(weights, inverse, grads):
         ratio, inside, sine, bend = waves(weights, inverse)
@@ -464,36 +544,6 @@
     def _(i):
         copy(sum_snd, sum_rcv.at[me], z_s, z_r, (me + i) % PEERS).start()
 
-    main_b, fold_b = unpack_tables(by_col[:, 4:6], None)
-    main_b, fold_b = terms(main_b, 1), terms(fold_b, 1)
-
-    def take_b(q):
-        grads = combined(1, q, main_b, fold_b)
-        g_wide[:, at(q, WIDTH)] = grads
-        return jnp.sum(xb[:, at(q, WIDTH)].astype(F32) * grads, axis=1, keepdims=True)
-
-    come_back(1, part, EXPERTS - 1)
-    along = take_b(part)
-
-    def body_b(s, total):
-        q = (part + s) % PARTS
-        come_back(1, q, EXPERTS)
-        return total + take_b(q)
-
-    along = lax.fori_loop(1, PARTS, body_b, along)
-    unit = unit_b[:, 0:1]
-    bent = along * unit * unit * unit * (1.0 / D)
-
-    @pl.loop(0, PARTS)
-    def _(q):
-        span = at(q, WIDTH)
-        back = g_wide[:, span] * unit - xb[:, span].astype(F32) * bent
-        out_b[:, span] = (cb[:, span].astype(F32) + back).astype(BF16)
-
-        @pl.when(pipe > 0)
-        def _():
-            copy(out_b.at[:, span], o_cot.at[:, span], p_s.at[1], p_r.at[1], me, pipe - 1).start()
-
     main_a, fold_a = unpack_tables(by_col[:, 0:2], by_col[:, 2:4])
     main_a, fold_a = terms(main_a, 3), terms(fold_a, 3)
 
@@ -505,14 +555,14 @@
         def _():
             copy(out_a.at[:, span], o_next.at[:, span], p_s.at[0], p_r.at[0], me, pipe + 1).start()
 
+    @pl.loop(1, PARTS)
+    def _(s):
+        q = (part + PARTS - s) % PARTS
+        come_back(0, q, EXPERTS)
+        take_a(q)
+
     come_back(0, part, EXPERTS - 1)
     take_a(part)
-
-    @pl.loop(1, PARTS)
-    def _(s):
-        q = (part + s) % PARTS
-        come_back(0, q, EXPERTS)
-        take_a(q)
 
     wait_for(sum_rcv.at[pl.ds(0, PEERS - 1)], z_r)
     for e in range(EXPERTS):
@@ -523,11 +573,17 @@
         wait_for(snd.at[slot, others_main], t_ss.at[slot])
         wait_for(snd_fold.at[slot, others_fold], t_sf.at[slot])
     for kind in (U, C, A):
-        wait_for(send1.at[kind], h_s.at[0, kind])
-        wait_for(send2.at[kind], h_s.at[1, kind])
-        wait_for(send3.at[kind], h_s.at[2, kind])
-        for step in range(3):
-            wait_for(gathered.at[kind, pl.ds(0, 1 << step)], g_s.at[step, kind])
+        wait_for(gathered.at[kind, pl.ds(0, 4)], c_s.at[kind])
+
+        @pl.when(is_end)
+        def _():
+            wait_for(send1.at[kind, pl.ds(0, 2)], l_s.at[kind])
+            wait_for(gathered.at[kind, pl.ds(0, 2)], g_s.at[kind])
+
+        @pl.when(jnp.logical_not(is_end))
+        def _():
+            wait_for(send1.at[kind], l_s.at[kind])
+            wait_for(gathered.at[kind, pl.ds(0, 4)], g_s.at[kind])
 
     @pl.when(pipe > 0)
     def _():
@@ -582,14 +638,13 @@
             bf(2, ROWS_MAIN, WIDTH), bf(2, FOLDED, 128),
             wide(2, 4, ROWS, 128),
             bf(3, 4, ROWS, 128), bf(3, 4, ROWS, 128),
-            bf(3, 2, ROWS, 128), bf(3, 2, ROWS, 128),
-            bf(3, ROWS, 128), bf(3, ROWS, 128),
+            bf(3, 4, ROWS, 128),
             bf(3, PARTS, ROWS, 128),
             bf(TOK, D), bf(TOK, D), wide(TOK, D),
             wide(TOK, 128), wide(TOK, 128),
             wide(8, 128), wide(PEERS, 8, 128),
             dma((2,)), dma((3,)), dma((2,)), dma((3,)),
-            dma((3, 3)), dma((3, 3)), dma((3, 3)), dma((3, 3)),
+            dma((3,)), dma((3,)), dma((3,)), dma((3, 4, 2)), dma((3,)), dma((3, 4, 2)), dma((3,)), dma((3,)),
             dma((2,)), dma((2, PARTS)), dma((2,)), dma((2, PARTS)),
             dma((2,)), dma((2,)), dma, dma,
         ],

time: 414 us -> 364 us (0.88)
  the two profiles are of different devices: /device:TPU:217 before, /device:TPU:16 now
where the time goes in v3:
time: 364 us
  Pallas kernels  352 us (97%)
  local copies, waits for them, and re-layouts  8.75 us (2%)
    pallas_call x1, Pallas kernels, shards(): pl.pallas_call(kernel, out_shape=(out(TOK, D), out(TOK, D), out(WIDTH, HI...  352 us

profile of v3, /device:TPU:16, one launch (start us, length us, event | category | flops | bytes accessed | tf_op | source)
XLA Modules:
  0.0 363.5 jit_solution(2428952950233022164)
XLA Ops:
  0.6 0.7 convert_bitcast_fusion
  1.3 1.3 pad_maximum_fusion
  2.6 0.7 copy.27.by_col
  3.3 352.1 %shard_map.154 = (bf16[64,7168]{1,0:T(8,128)(2,1)}, bf16[64,7168]{1,0:T(8,128)(2,1)}, bf16[896,1024]{1,0:T(8,128)(2,1)}, bf16[1024,896]{1,0:T(8,128)(2,1)}, f32[4,8,128]{2,1,0:T(8,128)}) custom-call(bf16[64,7168]{1,0:T(8,128)(2,1)} %bitcast.23, bf16[64,7168]{1,0:T(8,128)(2,1)} %bitcast.24, bf16[64,7168]{1,0:T(8,128)(2,1)} %bitcast.25, ...), custom_call_target="tpu_custom_call" | custom-call | tf_op jit(solution)/shard_map/pallas_call | solution.py:626
  355.4 0.0 copy-start.2
  355.4 1.4 slice_reduce_fusion
  356.9 0.0 copy-start.1
  356.9 2.3 copy.32
  359.2 0.0 copy-done.2
  359.2 0.9 copy.33
  360.1 0.0 copy-done.1
  360.1 0.0 copy-start
  360.1 1.2 copy.34
  361.3 0.9 copy-done
  362.3 1.2 copy.35
Async XLA Ops:
  355.4 3.8 %copy-start.2 = (bf16[64,7168]{1,0:T(8,128)(2,1)S(1)}, bf16[64,7168]{1,0:T(8,128)(2,1)}, u32[]{:S(2)}) copy-start(bf16[64,7168]{1,0:T(8,128)(2,1)} %get-tuple-element.12) | copy-start | bytes 2752516
  356.9 3.2 copy-start.1
  360.1 2.2 copy-start

commit v4 on v3

--- a/solution.py
+++ b/solution.py
@@ -133,11 +133,12 @@
 
 
 def kernel(
-    xa, xb, cb, by_row, by_col, w_up, w_down, s_up, s_down,
-    o_next, o_cot, o_up, o_down, o_sums,
+    xa_from, xb, cb_from, routes_a, gates_a, routes_b, gates_b, w_up_from, w_down_from, s_up, s_down,
+    o_next, o_cot, up_to, down_to, o_up_sums, o_down_sums,
+    xa, cb, w_up, w_down, o_up, o_down, i_s, o_s,
     q_up, q_down, rows, folds, snd, snd_fold, ret, ret_fold,
     keep, send1, recv1, passed, gathered,
-    out_a, out_b, g_wide, unit_a, unit_b, sum_snd, sum_rcv,
+    out_a, out_b, g_wide, unit_a, unit_b, up_total, down_total, sum_snd, sum_rcv,
     d_ss, d_rs, d_sf, d_rf, h_s, h_r, l_s, l_r, g_s, g_r, c_s, c_r, t_ss, t_rs, t_sf, t_rf, p_s, p_r, z_s, z_r,
 ):
     me = lax.axis_index("expert")
@@ -149,6 +150,15 @@
     upper = chip // 2
     is_end = (chip % 3) == 0
     over, away = me + 2 - 4 * upper, me - 2 + 4 * upper
+
+    loads = [
+        pltpu.make_async_copy(src, dst, i_s.at[i])
+        for i, (src, dst) in enumerate(
+            ((cb_from, cb), (w_up_from, w_up), (w_down_from, w_down), (xa_from, xa))
+        )
+    ]
+    for load in loads:
+        load.start()
 
     barrier = pltpu.get_barrier_semaphore()
 
@@ -387,13 +397,22 @@
         extra = sum(dot(table, fold) for table in foldeds)
         return total + jnp.concatenate([extra[b * TOK : (b + 1) * TOK] for b in range(BLOCKS)], axis=1)
 
-    table_b, gate_b = pack_tables(by_row[4:6, :], by_row[6:8, :])
+    by_row = jnp.concatenate(
+        (routes_a[...].astype(F32), gates_a[...], routes_b[...].astype(F32), gates_b[...]), axis=0
+    )
+    same = (iota((TOK, TOK), 0) == iota((TOK, TOK), 1)).astype(BF16)
+    by_col = sum(dot(same, term, NT) for term in terms(by_row, 3))
+    table_b, gate_b = pack_tables(by_row[4:6], by_row[6:8])
     norm_of(xb, unit_b)
     pl.semaphore_wait(
         barrier, PEERS - 1 + jnp.where(pipe > 0, 1, 0) + jnp.where(pipe < N_PIPE - 1, 1, 0)
     )
     dispatch(U, 0, xb, table_b, unit_b, None)
+    loads[0].wait()
     dispatch(C, 1, cb, table_b, None, gate_b)
+
+    for load in loads[1:]:
+        load.wait()
 
     step_up, step_down = s_up[0, mine], s_down[0, mine]
     one = jnp.ones((1, 1), F32)
@@ -409,7 +428,7 @@
         ratio, _, _, bend = waves(w_down[at(i, 64), :], inv_down)
         q_down[at(i, 64), :] = (step_down * (ratio - bend)).astype(BF16)
 
-    table_a, _ = pack_tables(by_row[0:2, :], by_row[2:4, :])
+    table_a, _ = pack_tables(by_row[0:2], by_row[2:4])
     norm_of(xa, unit_a)
 
     arrive(U)
@@ -474,35 +493,6 @@
     sent(0)
     give_back(0, lambda chunk: dot(wide(A, chunk), q_down[...]))
 
-    main_b, fold_b = unpack_tables(by_col[:, 4:6], None)
-    main_b, fold_b = terms(main_b, 1), terms(fold_b, 1)
-
-    def take_b(q):
-        grads = combined(1, q, main_b, fold_b)
-        g_wide[:, at(q, WIDTH)] = grads
-        return jnp.sum(xb[:, at(q, WIDTH)].astype(F32) * grads, axis=1, keepdims=True)
-
-    def body_b(s, total):
-        q = (part + PARTS - s) % PARTS
-        come_back(1, q, EXPERTS)
-        return total + take_b(q)
-
-    along = lax.fori_loop(1, PARTS, body_b, jnp.zeros((TOK, 1), F32))
-    come_back(1, part, EXPERTS - 1)
-    along = along + take_b(part)
-    unit = unit_b[:, 0:1]
-    bent = along * unit * unit * unit * (1.0 / D)
-
-    @pl.loop(0, PARTS)
-    def _(q):
-        span = at(q, WIDTH)
-        back = g_wide[:, span] * unit - xb[:, span].astype(F32) * bent
-        out_b[:, span] = (cb[:, span].astype(F32) + back).astype(BF16)
-
-        @pl.when(pipe > 0)
-        def _():
-            copy(out_b.at[:, span], o_cot.at[:, span], p_s.at[1], p_r.at[1], me, pipe - 1).start()
-
     def quant_grads(weights, inverse, grads):
         ratio, inside, sine, bend = waves(weights, inverse)
         wave = jnp.where(inside, 2.0 * sine * sine, 0.0)
@@ -511,30 +501,86 @@
             grads * (ratio - bend - ratio * wave), axis=0, keepdims=True
         )
 
-    def up_body(i, total):
+    def up_step(i):
         lhs = rows[U, :, at(i, 128)]
         for k in range(4):
             rhs = jnp.concatenate([gathered[U, 2 * k], gathered[U, 2 * k + 1]], axis=1)
             span = slice(k * 256, (k + 1) * 256)
             out, partial = quant_grads(w_up[at(i, 128), span], inv_up, dot(lhs, rhs, TN))
             o_up[at(i, 128), span] = out
-            total = total + partial
-        return total
-
-    def down_body(j, total):
+            up_total[:, span] = up_total[:, span] + partial
+
+    def down_step(j):
         out, partial = quant_grads(w_down[at(j, 128), :], inv_down, dot(gathered[C, j], rows[C], TN))
         o_down[at(j, 128), :] = out
-        return total + partial
-
-    up_total = lax.fori_loop(0, BLOCKS, up_body, jnp.zeros((1, 256), F32))
-    down_total = lax.fori_loop(0, PARTS, down_body, jnp.zeros((1, WIDTH), F32))
+        down_total[...] = down_total[...] + partial
+
+    up_total[...] = jnp.zeros_like(up_total)
+    down_total[...] = jnp.zeros_like(down_total)
+
+    @pl.loop(4, BLOCKS)
+    def _(i):
+        up_step(i)
+
+    main_b, fold_b = unpack_tables(by_col[:, 4:6], None)
+    main_b, fold_b = terms(main_b, 1), terms(fold_b, 1)
+
+    def take_b(q):
+        grads = combined(1, q, main_b, fold_b)
+        g_wide[:, at(q, WIDTH)] = grads
+        return jnp.sum(xb[:, at(q, WIDTH)].astype(F32) * grads, axis=1, keepdims=True)
+
+    def body_b(s, total):
+        q = (part + PARTS - s) % PARTS
+        come_back(1, q, EXPERTS)
+        return total + take_b(q)
+
+    along = lax.fori_loop(1, PARTS, body_b, jnp.zeros((TOK, 1), F32))
+    come_back(1, part, EXPERTS - 1)
+    along = along + take_b(part)
+    unit = unit_b[:, 0:1]
+    bent = along * unit * unit * unit * (1.0 / D)
+
+    @pl.loop(0, PARTS)
+    def _(q):
+        span = at(q, WIDTH)
+        back = g_wide[:, span] * unit - xb[:, span].astype(F32) * bent
+        out_b[:, span] = (cb[:, span].astype(F32) + back).astype(BF16)
+
+        @pl.when(pipe > 0)
+        def _():
+            copy(out_b.at[:, span], o_cot.at[:, span], p_s.at[1], p_r.at[1], me, pipe - 1).start()
+
+    main_a, fold_a = unpack_tables(by_col[:, 0:2], by_col[:, 2:4])
+    main_a, fold_a = terms(main_a, 3), terms(fold_a, 3)
+
+    def take_a(q):
+        span = at(q, WIDTH)
+        out_a[:, span] = (xa[:, span].astype(F32) + combined(0, q, main_a, fold_a)).astype(BF16)
+
+        @pl.when(pipe < N_PIPE - 1)
+        def _():
+            copy(out_a.at[:, span], o_next.at[:, span], p_s.at[0], p_r.at[0], me, pipe + 1).start()
+
+    @pl.loop(1, 5)
+    def _(s):
+        up_step(s - 1)
+        down_step(2 * s - 2)
+        down_step(2 * s - 1)
+        q = (part + PARTS - s) % PARTS
+        come_back(0, q, EXPERTS)
+        take_a(q)
+
+    stores = [pltpu.make_async_copy(o_up, up_to, o_s.at[0]), pltpu.make_async_copy(o_down, down_to, o_s.at[1])]
+    for store in stores:
+        store.start()
     first = iota((8, 128), 0) == 0
     scaled = 1.0 / math.sqrt(D * HID * qlimit)
     sum_snd[...] = (
         jnp.where(
             first,
-            jnp.sum(up_total, axis=1, keepdims=True),
-            jnp.sum(down_total, axis=1, keepdims=True),
+            jnp.sum(up_total[...], axis=1, keepdims=True),
+            jnp.sum(down_total[...], axis=1, keepdims=True),
         )
         * scaled
     )
@@ -544,18 +590,7 @@
     def _(i):
         copy(sum_snd, sum_rcv.at[me], z_s, z_r, (me + i) % PEERS).start()
 
-    main_a, fold_a = unpack_tables(by_col[:, 0:2], by_col[:, 2:4])
-    main_a, fold_a = terms(main_a, 3), terms(fold_a, 3)
-
-    def take_a(q):
-        span = at(q, WIDTH)
-        out_a[:, span] = (xa[:, span].astype(F32) + combined(0, q, main_a, fold_a)).astype(BF16)
-
-        @pl.when(pipe < N_PIPE - 1)
-        def _():
-            copy(out_a.at[:, span], o_next.at[:, span], p_s.at[0], p_r.at[0], me, pipe + 1).start()
-
-    @pl.loop(1, PARTS)
+    @pl.loop(5, PARTS)
     def _(s):
         q = (part + PARTS - s) % PARTS
         come_back(0, q, EXPERTS)
@@ -565,10 +600,16 @@
     take_a(part)
 
     wait_for(sum_rcv.at[pl.ds(0, PEERS - 1)], z_r)
+    lane = iota((8, 128), 1)
+    sums = jnp.zeros((8, 128), F32)
     for e in range(EXPERTS):
-        o_sums[e] = sum(sum_rcv[e * PARTS + k] for k in range(PARTS))
+        sums = jnp.where(lane == e, sum(sum_rcv[e * PARTS + k] for k in range(PARTS)), sums)
+    o_up_sums[...] = sums[0:1, :EXPERTS]
+    o_down_sums[...] = sums[1:2, :EXPERTS]
 
     wait_for(sum_rcv.at[pl.ds(0, PEERS - 1)], z_s)
+    for store in stores:
+        store.wait()
     for slot in (0, 1):
         wait_for(snd.at[slot, others_main], t_ss.at[slot])
         wait_for(snd_fold.at[slot, others_fold], t_sf.at[slot])
@@ -607,10 +648,8 @@
 def shards(
     acts_a, acts_b, cot_b, routes_a, gates_a, routes_b, gates_b, up_weight, down_weight, up_scale, down_scale
 ):
-    by_col = jnp.concatenate(
-        (routes_a[0].astype(F32), gates_a[0], routes_b[0].astype(F32), gates_b[0]), axis=1
-    )
     vmem = pl.BlockSpec(memory_space=pltpu.VMEM)
+    hbm = pl.BlockSpec(memory_space=pl.ANY)
     smem = pl.BlockSpec(memory_space=pltpu.SMEM)
     dma = pltpu.SemaphoreType.DMA
 
@@ -623,15 +662,17 @@
     def out(*shape):
         return jax.ShapeDtypeStruct(shape, BF16)
 
-    next_a, next_cot, dw_up, dw_down, sums = pl.pallas_call(
+    made = pl.pallas_call(
         kernel,
         out_shape=(
             out(TOK, D), out(TOK, D), out(WIDTH, HID), out(HID, WIDTH),
-            jax.ShapeDtypeStruct((EXPERTS, 8, 128), F32),
+            jax.ShapeDtypeStruct((1, EXPERTS), F32), jax.ShapeDtypeStruct((1, EXPERTS), F32),
         ),
-        in_specs=[vmem] * 7 + [smem] * 2,
-        out_specs=(vmem,) * 5,
+        in_specs=[hbm, vmem, hbm, vmem, vmem, vmem, vmem, hbm, hbm, smem, smem],
+        out_specs=(vmem, vmem, hbm, hbm, vmem, vmem),
         scratch_shapes=[
+            bf(TOK, D), bf(TOK, D), bf(WIDTH, HID), bf(HID, WIDTH), bf(WIDTH, HID), bf(HID, WIDTH),
+            dma((4,)), dma((2,)),
             bf(WIDTH, HID), bf(HID, WIDTH),
             bf(3, ROWS, WIDTH), bf(3, FOLDED, 128),
             bf(2, ROWS_MAIN, WIDTH), bf(2, FOLDED, 128),
@@ -642,7 +683,7 @@
             bf(3, PARTS, ROWS, 128),
             bf(TOK, D), bf(TOK, D), wide(TOK, D),
             wide(TOK, 128), wide(TOK, 128),
-            wide(8, 128), wide(PEERS, 8, 128),
+            wide(1, HID), wide(1, WIDTH), wide(8, 128), wide(PEERS, 8, 128),
             dma((2,)), dma((3,)), dma((2,)), dma((3,)),
             dma((3,)), dma((3,)), dma((3,)), dma((3, 4, 2)), dma((3,)), dma((3, 4, 2)), dma((3,)), dma((3,)),
             dma((2,)), dma((2, PARTS)), dma((2,)), dma((2, PARTS)),
@@ -652,11 +693,10 @@
             collective_id=0, has_side_effects=True, vmem_limit_bytes=62 << 20
         ),
     )(
-        acts_a[0], acts_b[0], cot_b[0], by_col.T, by_col, up_weight[0], down_weight[0], up_scale, down_scale
+        acts_a[0], acts_b[0], cot_b[0], routes_a[0].T, gates_a[0].T, routes_b[0].T, gates_b[0].T, up_weight[0], down_weight[0], up_scale, down_scale
     )
-    return (
-        next_a[None], next_cot[None], dw_up[None], dw_down[None], sums[None, :, 0, 0], sums[None, :, 1, 0],
-    )
+    next_a, next_cot, dw_up, dw_down, up_sums, down_sums = made
+    return (next_a[None], next_cot[None], dw_up[None], dw_down[None], up_sums, down_sums)
 
 
 def solution(mesh):

time: 364 us -> 361 us (level)
    unnamed x10 -> x16, local copies, waits for them, and re-layouts: 6.61 us -> 7.66 us
where the time goes in v4:
time: 361 us; the launch traced here: 360 us
  Pallas kernels  351 us (97%)
  local copies, waits for them, and re-layouts  7.66 us (2%)
    pallas_call x1, Pallas kernels, shards(): pl.pallas_call(kernel, out_shape=(out(TOK, D), out(TOK, D), out(WIDTH, HI...  351 us
    unnamed x16, local copies, waits for them, and re-layouts  7.66 us

profile of v4, /device:TPU:16, one launch (start us, length us, event | category | flops | bytes accessed | tf_op | source)
XLA Modules:
  0.0 359.7 jit_solution(9751200570656248960)
XLA Ops:
  0.6 351.4 %shard_map.154 = (bf16[64,7168]{1,0:T(8,128)(2,1)}, bf16[64,7168]{1,0:T(8,128)(2,1)}, bf16[896,1024]{1,0:T(8,128)(2,1)}, bf16[1024,896]{1,0:T(8,128)(2,1)}, f32[1,4]{1,0:T(1,128)}, /*index=5*/f32[1,4]{1,0:T(1,128)}) custom-call(bf16[64,7168]{1,0:T(8,128)(2,1)} %bitcast.25, bf16[64,7168]{1,0:T(8,128)(2,1)} %bitcast.26, bf16[64,7168]{1,0:T(8,128)(2,1)} %bitcast.27, ...), custom_call_target="tpu_custom_call" | custom-call | tf_op jit(solution)/shard_map/pallas_call | solution.py:665
  352.0 0.0 copy-start.2
  352.0 0.0 copy-start.1
  352.0 2.3 copy.23
  354.3 0.0 copy-done.2
  354.3 0.9 copy.24
  355.3 0.0 copy-done.1
  355.3 0.0 copy-start
  355.3 1.2 copy.25
  356.5 0.9 copy-done
  357.4 0.0 copy-start.4
  357.4 0.0 copy-start.3
  357.4 1.2 copy.26
  358.7 0.0 copy-done.4
  358.7 0.5 copy.27
  359.2 0.0 copy-done.3
  359.2 0.5 copy.28
Async XLA Ops:
  352.0 2.3 copy-start.2
  352.0 3.2 copy-start.1
  355.3 2.2 copy-start
  357.4 1.2 copy-start.4
  357.4 1.7 copy-start.3
